TPU v7x, 128 devices: a whole 4x4x4 slice. The times are simulated.
128 devices in a mesh: row: 8 (over z, x_lo), col: 16 (over x_hi, y, core).
Axes of the slice: x: 4 (x_hi: 2, x_lo: 2; x = x_hi * 2 + x_lo), y: 4, z: 4, core: 2. Of those that a mesh axis runs over, the one named last changes fastest.
Arguments:
- frames: bfloat16 [2, 1024, 1024, 128], P(None, 'row', 'col'), may hold values from -6 to 6
- conv_weight: bfloat16 [3, 3, 128, 128], replicated, may hold values from -0.1875 to 0.1875
- embed_weight: bfloat16 [32768, 2048], P('row', 'col'), may hold values from -0.03125 to 0.03125
- unembed_weight: bfloat16 [32768, 2048], P('row', 'col'), may hold values from -0.125 to 0.125
- qkv_weight: bfloat16 [3, 2048, 2048], P(None, None, 'col'), may hold values from -0.261584 to 0.261584
- out_weight: bfloat16 [2048, 2048], P('col'), may hold values from -0.125 to 0.125
Outputs:
- denoised: bfloat16 [2, 1024, 1024, 128], P(None, 'row', 'col')
All inputs are finite; a program needn't handle non-finite values.
Results may differ from a plain program's by a relative error of at most 0.025.
Values may be sent and summed in bfloat16 or wider, within the bound.
No kernel may reach another device: no remote copies, remote signals or barrier semaphores. Data moves between devices by JAX's collectives and lax.ppermute only.
A program may use at most 128 MiB of HBM per device.

v0:
```python
import functools

import jax
import jax.numpy as jnp
from jax import lax
from jax.experimental import pallas as pl
from jax.experimental.pallas import tpu as pltpu
from jax.sharding import PartitionSpec as P

C = 128
BF = jnp.bfloat16
F32 = jnp.float32
EPS = 1e-06
ROW = ("z", "xl")
COL = ("xh", "y", "core")
ROWY = ROW + ("y",)
SAME = ROW + ("xh", "y")
EVERY = ROW + COL
CHUNK = 64
SPREAD = 64
SUB = 16
LEFT = 8


def params(mib=12):
    return pltpu.CompilerParams(vmem_limit_bytes=mib * 2**20)


def near(*arrays):
    return [pltpu.with_memory_space_constraint(array, pltpu.VMEM) for array in arrays]


VMEM = pl.BlockSpec(memory_space=pltpu.VMEM)


def conv_kernel(
    main, above, below, top, bottom, left, right, weight, features, send, padded, taps, kernel, pooled
):
    frame, step = pl.program_id(0), pl.program_id(1)

    @pl.when((frame == 0) & (step == 0))
    def _():
        for a in range(3):
            for k in range(4):
                for o in range(2):
                    b = k - o
                    block = weight[a, b] if 0 <= b <= 2 else jnp.zeros((C, C), BF)
                    kernel[pl.ds(a * 512 + k * C, C), pl.ds(o * C, C)] = block

    cols = pl.ds(LEFT, 64)
    start = step * CHUNK
    padded[pl.ds(1, CHUNK), cols, :] = main[0].astype(F32)
    rows = pl.ds(pl.multiple_of(start, CHUNK), CHUNK)
    padded[pl.ds(1, CHUNK), LEFT - 1, :] = left[frame, rows, :].astype(F32)
    padded[pl.ds(1, CHUNK), LEFT + 64, :] = right[frame, rows, :].astype(F32)
    for border, outside, inside, row, at in (
        (step == 0, top, above, CHUNK - 1, 0),
        (step == 1, bottom, below, CHUNK, CHUNK + 1),
    ):

        @pl.when(border)
        def _(outside=outside, at=at):
            padded[at, cols, :] = outside[frame, pl.ds(0, 64)].astype(F32)
            corners = outside[frame, pl.ds(64, 16)].astype(F32)
            padded[at, pl.ds(LEFT - 1, 1), :] = corners[:1]
            padded[at, pl.ds(LEFT + 64, 1), :] = corners[1:2]

        @pl.when(jnp.logical_not(border))
        def _(inside=inside, row=row, at=at):
            padded[at, cols, :] = inside[0, 0].astype(F32)
            near_row = pl.ds(row // 16 * 16, 16)
            for side, col in ((left, LEFT - 1), (right, LEFT + 64)):
                value = side[frame, near_row, :].astype(F32)
                padded[at, pl.ds(col, 1), :] = value[row % 16 : row % 16 + 1]

    for k in range(6):
        taps[:, :, pl.ds(k * C, C)] = padded[:, pl.ds(LEFT - 1 + k, 16, stride=4), :].astype(BF)

    for sub in range(CHUNK // SUB):
        total = jnp.zeros((SUB // 4, 16, C), F32)
        for pair in range(2):
            lhs = jnp.concatenate(
                [
                    taps[pl.ds(sub * SUB + a, SUB), :, pl.ds(pair * 256, 512)].reshape(SUB * 16, 512)
                    for a in range(3)
                ],
                axis=1,
            )
            result = jnp.dot(lhs, kernel[...], preferred_element_type=F32)
            for o in range(2):
                m = pair * 2 + o
                v = result[:, o * C : (o + 1) * C]
                mean = jnp.mean(v * v, axis=-1, keepdims=True)
                h = v * (0.5 * lax.rsqrt(mean + EPS))
                x = taps[pl.ds(sub * SUB + 1, SUB), :, pl.ds((m + 1) * C, C)].reshape(SUB * 16, C)
                f = x.astype(F32) + (h + h * jnp.tanh(h))
                f = f.reshape(SUB, 16, C)
                features[0, pl.ds(sub * SUB, SUB), m] = f.astype(BF)
                total = total + f.reshape(SUB // 4, 4, 16, C).sum(axis=1)
        mean = total * (1.0 / 16.0)
        for g in range(SUB // 4):
            q = sub * (SUB // 4) + g
            token = frame * 2 + step
            for half in range(2):
                piece = q * 2 + half
                at = pl.ds(pl.multiple_of(token * 8, 8), 8)
                pooled[piece, at, :] = mean[g, half * 8 : half * 8 + 8]

    @pl.when((frame == 1) & (step == 1))
    def _():
        for r in range(8):
            for y in range(4):
                block = pooled[r * 4 + y].astype(BF)
                for xh in range(2):
                    send[(r * 2 + xh) * 4 + y] = block


def convolve(frames, top, bottom, left, right, weight):
    steps = 128 // CHUNK
    far = pltpu.with_memory_space_constraint(frames, pltpu.HBM)
    return pl.pallas_call(
        conv_kernel,
        grid=(2, steps),
        in_specs=[
            pl.BlockSpec((1, CHUNK, 64, C), lambda f, i: (f, i, 0, 0)),
            pl.BlockSpec((1, 1, 64, C), lambda f, i: (f, CHUNK - 1, 0, 0)),
            pl.BlockSpec((1, 1, 64, C), lambda f, i: (f, CHUNK, 0, 0)),
        ]
        + [VMEM] * 5,
        out_specs=[pl.BlockSpec((1, CHUNK, 4, 16, C), lambda f, i: (f, i, 0, 0, 0)), VMEM],
        out_shape=[
            pltpu.HBM((2, 128, 4, 16, C), BF),
            pltpu.VMEM((64, 32, C), BF),
        ],
        scratch_shapes=[
            pltpu.VMEM((CHUNK + 2, 80, C), F32),
            pltpu.VMEM((CHUNK + 2, 16, 6 * C), BF),
            pltpu.VMEM((3 * 512, 2 * C), BF),
            pltpu.VMEM((32, 32, C), F32),
        ],
        compiler_params=params(),
        cost_estimate=pl.CostEstimate(
            flops=2 * 16384 * 9 * C * C, bytes_accessed=9 * 2**20, transcendentals=2 * 16384 * C
        ),
        name="conv_block",
    )(far, far, far, *near(top, bottom, left, right, weight))


def embed_kernel(received, own, other, out, rows, values, wide):
    core = lax.axis_index("core")
    rows[...] = received[...].reshape(2048, C).astype(F32)
    for j in range(8):
        values[:, pl.ds(j * C, C)] = rows[pl.ds(j, 256, stride=8), :].astype(BF)
    for which, weight in enumerate((own, other)):
        for y in range(4):
            wide[:, pl.ds(y * C, C)] = weight[y, pl.ds(0, 1024)]
        result = jnp.dot(values[...], wide[...], preferred_element_type=F32).astype(BF)
        feature = core if which == 0 else 1 - core
        for r in range(8):
            for y in range(4):
                out[r * 4 + y, feature] = result[r * 32 : r * 32 + 32, y * C : y * C + C]


def embed(received, own, other):
    return pl.pallas_call(
        embed_kernel,
        out_shape=pltpu.VMEM((32, 2, 32, C), BF),
        scratch_shapes=[
            pltpu.VMEM((2048, C), F32),
            pltpu.VMEM((256, 1024), BF),
            pltpu.VMEM((1024, 512), BF),
        ],
        compiler_params=params(),
        name="embed",
    )(*near(received, own, other))


def sum_kernel(copies, terms, *rest):
    out, total_out = rest[-2:]
    total = terms[0].astype(F32)
    for i in range(1, terms.shape[0]):
        total = total + terms[i].astype(F32)
    if len(rest) == 3:
        total = rest[0][...].astype(F32) + total
    total = total.astype(BF)
    total_out[...] = total
    for i in range(copies):
        out[i] = total


def sum_and_copy(copies, terms, *base):
    return pl.pallas_call(
        functools.partial(sum_kernel, copies),
        out_shape=[pltpu.VMEM((copies, 2, 32, C), BF), pltpu.VMEM((2, 32, C), BF)],
        compiler_params=params(),
        name="sum_and_copy",
    )(*near(terms, *base))


def qkv_kernel(embedded, weight, queries, pairs):
    normed = []
    for core in range(2):
        blocks = [
            embedded[pair * 2 + core, feature].astype(F32)
            for pair in range(8)
            for feature in range(2)
        ]
        square = sum(block * block for block in blocks)
        square = jnp.sum(square, axis=-1, keepdims=True)
        scale = lax.rsqrt(square * (1.0 / 2048.0) + EPS)
        normed.append(jnp.concatenate([(block * scale).astype(BF) for block in blocks], axis=1))
    normed = jnp.concatenate(normed, axis=0)
    queries[...] = jnp.dot(normed, weight[0], preferred_element_type=F32).astype(BF)
    for part in range(2):
        result = jnp.dot(normed, weight[1 + part], preferred_element_type=F32).astype(BF)
        for r in range(8):
            pairs[r, part] = result


def project_qkv(embedded, weight):
    return pl.pallas_call(
        qkv_kernel,
        out_shape=[pltpu.VMEM((64, C), BF), pltpu.VMEM((8, 2, 64, C), BF)],
        compiler_params=params(),
        name="qkv",
    )(*near(embedded, weight))


def attend_kernel(queries, pairs, weight, out):
    keys = pairs[:, 0].reshape(512, C)
    values = pairs[:, 1].reshape(512, C)
    scores = lax.dot_general(
        queries[...], keys, (((1,), (1,)), ((), ())), preferred_element_type=F32
    ) * C ** (-0.5)
    scores = jnp.exp(scores - jnp.max(scores, axis=-1, keepdims=True))
    weights = (scores / jnp.sum(scores, axis=-1, keepdims=True)).astype(BF)
    attended = jnp.dot(weights, values, preferred_element_type=F32).astype(BF)
    projected = jnp.dot(attended, weight[...], preferred_element_type=F32).astype(BF)
    for pair in range(8):
        for core in range(2):
            for feature in range(2):
                at = (pair * 2 + feature) * C
                out[pair * 2 + core, feature] = projected[core * 32 : core * 32 + 32, at : at + C]


def attend(queries, pairs, weight):
    return pl.pallas_call(
        attend_kernel,
        out_shape=pltpu.VMEM((16, 2, 32, C), BF),
        compiler_params=params(),
        name="attend",
    )(*near(queries, pairs, weight))


def unembed_kernel(mixed, own, other, out, values, wide, rows):
    core = lax.axis_index("core")
    for which, weight in enumerate((own, other)):
        feature = core if which == 0 else 1 - core
        for y in range(4):
            at = pl.ds((which * 4 + y) * C, C)
            wide[:, at] = weight[y, pl.ds(1024, 1024)]
            for r in range(8):
                values[pl.ds(r * 32, 32), at] = mixed[r * 4 + y, feature]
    for j in range(8):
        rows[pl.ds(j, 256, stride=8), :] = lax.dot_general(
            values[...],
            wide[pl.ds(j * C, C), :],
            (((1,), (1,)), ((), ())),
            preferred_element_type=F32,
        )
    out[...] = rows[...].astype(BF).reshape(64, 32, C)


def unembed(mixed, own, other):
    return pl.pallas_call(
        unembed_kernel,
        out_shape=pltpu.VMEM((64, 32, C), BF),
        scratch_shapes=[
            pltpu.VMEM((256, 1024), BF),
            pltpu.VMEM((1024, 1024), BF),
            pltpu.VMEM((2048, C), F32),
        ],
        compiler_params=params(),
        name="unembed",
    )(*near(mixed, own, other))


def finish_kernel(features, received, out, patch, spread):
    frame, step = pl.program_id(0), pl.program_id(1)

    @pl.when((frame == 0) & (step == 0))
    def _():
        for r in range(8):
            for y in range(4):
                total = received[r * 8 + y].astype(F32) + received[r * 8 + 4 + y].astype(F32)
                patch[r * 4 + y] = total.astype(BF).astype(F32)

    token = frame * 2 + step
    at = pl.ds(pl.multiple_of(token * 8, 8), 8)
    for q in range(SPREAD // 4):
        piece = q * 2
        small = jnp.concatenate([patch[piece, at, :], patch[piece + 1, at, :]], axis=0)
        for row in range(4):
            for m in range(4):
                value = features[frame, step * SPREAD + q * 4 + row, m].astype(F32) + small
                spread[q * 4 + row, pl.ds(m, 16, stride=4), :] = value
    out[0] = spread[...].astype(BF)


def finish(features, received):
    return pl.pallas_call(
        finish_kernel,
        grid=(2, 128 // SPREAD),
        in_specs=[VMEM, VMEM],
        out_specs=pl.BlockSpec((1, SPREAD, 64, C), lambda f, i: (f, i, 0, 0)),
        out_shape=jax.ShapeDtypeStruct((2, 128, 64, C), BF),
        scratch_shapes=[
            pltpu.VMEM((32, 32, C), F32),
            pltpu.VMEM((SPREAD, 64, C), F32),
        ],
        compiler_params=params(),
        name="finish",
    )(*near(features, received))


def exchange(array, axes):
    return lax.all_to_all(array, axes, 0, 0, tiled=True)


def from_neighbours(low, high, axes, count):
    forward = [(i, i + 1) for i in range(count - 1)]
    backward = [(i + 1, i) for i in range(count - 1)]
    return lax.ppermute(low, axes, forward), lax.ppermute(high, axes, backward)


def on_device(frames, conv_weight, embed_weight, unembed_weight, qkv_weight, out_weight):
    left, right = from_neighbours(frames[:, :, 63], frames[:, :, 0], COL, 16)
    both = [weight.reshape(4, 1024, C) for weight in (embed_weight, unembed_weight)]
    both = jnp.concatenate(both, axis=1)
    left, right, both = lax.optimization_barrier((left, right, both))
    rows = [
        jnp.pad(
            jnp.concatenate([frames[:, y], left[:, y : y + 1], right[:, y : y + 1]], axis=1),
            ((0, 0), (0, 14), (0, 0)),
        )
        for y in (127, 0)
    ]
    top, bottom = from_neighbours(rows[0], rows[1], ROW, 8)
    own = exchange(both, "y")
    features, patches = convolve(frames, top, bottom, left, right, conv_weight)
    own, patches = lax.optimization_barrier((own, patches))
    other = lax.ppermute(own, "core", [(0, 1), (1, 0)])
    partial = embed(exchange(patches, SAME), own, other)
    copies, embedded = sum_and_copy(16, exchange(partial, ROWY))
    queries, pairs = project_qkv(exchange(copies, COL), qkv_weight)
    projected = attend(queries, exchange(pairs, ROW), out_weight)
    copies, _ = sum_and_copy(32, exchange(projected, COL), embedded)
    patch_values = unembed(exchange(copies, ROWY), own, other)
    return finish(features, exchange(patch_values, SAME))


def solution(mesh):
    fine = jax.sharding.Mesh(mesh.devices.reshape(4, 2, 2, 4, 2), EVERY)
    placed = (
        P(None, ROW, COL, None),
        P(),
        P(ROW, COL),
        P(ROW, COL),
        P(None, None, COL),
        P(COL, None),
    )
    return jax.shard_map(
        on_device,
        mesh=fine,
        in_specs=placed,
        out_specs=P(None, ROW, COL, None),
        check_vma=False,
    )
```

profile of v0, /device:TPU:0, one launch (start us, length us, event | category | flops | bytes accessed | tf_op | source)
XLA Modules:
  0.0 157.2 jit_solution(12520220691044328048)
XLA Ops:
  0.0 1.4 fusion.10
  1.4 1.3 collective-permute-start
  2.8 1.3 collective-permute-start.1
  4.1 0.0 copy-start.3
  4.1 3.1 %pad_maximum_fusion = bf16[4,2048,128]{2,1,0:T(8,128)(2,1)} fusion(bf16[4,1024,128]{2,1,0:T(8,128)(2,1)} %bitcast.16, bf16[4,1024,128]{2,1,0:T(8,128)(2,1)} %bitcast.17), kind=kLoop, calls=%fused_computation | loop fusion | flops 4194304 | bytes 4194304 | tf_op jit(solution)/shard_map/concatenate | solution.py:339
  7.1 0.0 collective-permute-done.left
  7.1 0.7 collective-permute-done.1.right
  7.8 6.9 %all-to-all-start = ((bf16[4,2048,128]{2,1,0:T(8,128)(2,1)}), bf16[4,2048,128]{2,1,0:T(8,128)(2,1)S(1)}, u32[]{:S(2)}, u32[]{:S(2)}) async-start(bf16[4,2048,128]{2,1,0:T(8,128)(2,1)} %pad_maximum_fusion), calls=%async_computation | async-start | bytes 4194304 | tf_op jit(solution)/shard_map/all_to_all | solution.py:327
  14.7 0.8 slice_bitcast_fusion
  15.5 3.4 %collective-permute-start.2 = (bf16[2,80,128]{2,1,0:T(8,128)(2,1)S(1)}, bf16[2,80,128]{2,1,0:T(8,128)(2,1)S(1)}, u32[]{:S(2)}, u32[]{:S(2)}) collective-permute-start(bf16[2,80,128]{2,1,0:T(8,128)(2,1)S(1)} %fusion.7), channel_id=1, source_target_pairs={{0,16},{16,32},{32,48},{48,64},{64,80},{80,96},{96,112},{1,17},{17... | collective-permute-start | bytes 122888 | tf_op jit(solution)/shard_map/ppermute | solution.py:333
  18.9 1.3 collective-permute-start.3
  20.2 0.3 collective-permute-done.2.top
  20.5 4.3 %collective-permute-done.3.bottom = bf16[2,80,128]{2,1,0:T(8,128)(2,1)S(1)} collective-permute-done((bf16[2,80,128]{2,1,0:T(8,128)(2,1)S(1)}, bf16[2,80,128]{2,1,0:T(8,128)(2,1)S(1)}, u32[]{:S(2)}, u32[]{:S(2)}) %collective-permute-start.3) | collective-permute-done | bytes 40992 | tf_op jit(solution)/shard_map/ppermute | solution.py:333
  24.8 0.0 copy-done.3
  24.8 12.4 %conv_block.1 = (bf16[2,128,4,16,128]{4,3,2,1,0:T(8,128)(2,1)}, bf16[64,32,128]{2,1,0:T(8,128)(2,1)S(1)}) custom-call(bf16[2,128,64,128]{3,2,1,0:T(8,128)(2,1)} %below.1, bf16[2,128,64,128]{3,2,1,0:T(8,128)(2,1)} %below.1, bf16[2,128,64,128]{3,2,1,0:T(8,128)(2,1)} %below.1, bf16[2,80,128]{2,1,0:T(8,128)(2,1)S(1)} %collective-permute-done.2.top, ...), custom_call_target="tpu_custom_call" | custom-call | flops 4831838208 | bytes 9437184 | tf_op jit(solution)/shard_map/conv_block/pallas_call | solution.py:121
  37.2 1.4 all-to-all-done.own
  38.5 0.0 copy-start.1
  38.5 3.7 %collective-permute-start.4 = (bf16[4,2048,128]{2,1,0:T(8,128)(2,1)S(1)}, bf16[4,2048,128]{2,1,0:T(8,128)(2,1)S(1)}, u32[]{:S(2)}, u32[]{:S(2)}) collective-permute-start(bf16[4,2048,128]{2,1,0:T(8,128)(2,1)S(1)} %all-to-all-done.own), channel_id=1, source_target_pairs={{0,1},{1,0},{2,3},{3,2},{4,5},{5,4},{6,7},{7,6},{8,9},{9,8},{10,11... | collective-permute-start | bytes 6291464 | tf_op jit(solution)/shard_map/ppermute | solution.py:352
  42.2 23.9 %all_to_all.40.received = bf16[64,32,128]{2,1,0:T(8,128)(2,1)S(1)} all-to-all(bf16[64,32,128]{2,1,0:T(8,128)(2,1)S(1)} %get-tuple-element.22), channel_id=1, replica_groups=mesh['z'=4,'xl'=2,'xh'=2,'y'=4,'core'=2] {'z','xl','xh','y'}, dimensions={0} | all-to-all | bytes 1048576 | tf_op jit(solution)/shard_map/all_to_all | solution.py:327
  66.2 0.0 copy-start.2
  66.2 0.0 collective-permute-done.4.other
  66.2 1.2 embed.1
  67.4 14.0 %all_to_all.41.terms = bf16[32,2,32,128]{3,2,1,0:T(8,128)(2,1)S(1)} all-to-all(bf16[32,2,32,128]{3,2,1,0:T(8,128)(2,1)S(1)} %embed.1), channel_id=1, replica_groups=mesh['z'=4,'xl'=2,'xh'=2,'y'=4,'core'=2] {'z','xl','y'}, dimensions={0} | all-to-all | bytes 1048576 | tf_op jit(solution)/shard_map/all_to_all | solution.py:327
  81.4 0.1 sum_and_copy.2
  81.5 14.2 %all_to_all.42.embedded = bf16[16,2,32,128]{3,2,1,0:T(8,128)(2,1)S(1)} all-to-all(bf16[16,2,32,128]{3,2,1,0:T(8,128)(2,1)S(1)} %get-tuple-element.24), channel_id=1, replica_groups=mesh['z'=4,'xl'=2,'xh'=2,'y'=4,'core'=2] {'xh','y','core'}, dimensions={0} | all-to-all | bytes 524288 | tf_op jit(solution)/shard_map/all_to_all | solution.py:327
  95.7 0.0 copy-done.1
  95.7 0.5 qkv.1
  96.2 9.7 %all_to_all.43.pairs = bf16[8,2,64,128]{3,2,1,0:T(8,128)(2,1)S(1)} all-to-all(bf16[8,2,64,128]{3,2,1,0:T(8,128)(2,1)S(1)} %get-tuple-element.26), channel_id=1, replica_groups=mesh['z'=4,'xl'=2,'xh'=2,'y'=4,'core'=2] {'z','xl'}, dimensions={0} | all-to-all | bytes 524288 | tf_op jit(solution)/shard_map/all_to_all | solution.py:327
  105.8 0.0 copy-done.2
  105.9 0.7 attend.1
  106.5 0.0 copy-start
  106.5 12.8 %all_to_all.44.terms = bf16[16,2,32,128]{3,2,1,0:T(8,128)(2,1)S(1)} all-to-all(bf16[16,2,32,128]{3,2,1,0:T(8,128)(2,1)S(1)} %attend.1), channel_id=1, replica_groups=mesh['z'=4,'xl'=2,'xh'=2,'y'=4,'core'=2] {'xh','y','core'}, dimensions={0} | all-to-all | bytes 524288 | tf_op jit(solution)/shard_map/all_to_all | solution.py:327
  119.3 0.7 sum_and_copy.3
  120.0 15.0 %all_to_all.45.mixed = bf16[32,2,32,128]{3,2,1,0:T(8,128)(2,1)S(1)} all-to-all(bf16[32,2,32,128]{3,2,1,0:T(8,128)(2,1)S(1)} %get-tuple-element.28), channel_id=1, replica_groups=mesh['z'=4,'xl'=2,'xh'=2,'y'=4,'core'=2] {'z','xl','y'}, dimensions={0} | all-to-all | bytes 1048576 | tf_op jit(solution)/shard_map/all_to_all | solution.py:327
  135.0 1.4 unembed.1
  136.4 17.9 %all_to_all.46.received = bf16[64,32,128]{2,1,0:T(8,128)(2,1)S(1)} all-to-all(bf16[64,32,128]{2,1,0:T(8,128)(2,1)S(1)} %unembed.1), channel_id=1, replica_groups=mesh['z'=4,'xl'=2,'xh'=2,'y'=4,'core'=2] {'z','xl','xh','y'}, dimensions={0} | all-to-all | bytes 1048576 | tf_op jit(solution)/shard_map/all_to_all | solution.py:327
  154.3 0.0 copy-done
  154.3 2.8 %finish.1 = bf16[2,128,64,128]{3,2,1,0:T(8,128)(2,1)} custom-call(bf16[2,128,4,16,128]{4,3,2,1,0:T(8,128)(2,1)S(1)} %copy-done, bf16[64,32,128]{2,1,0:T(8,128)(2,1)S(1)} %all_to_all.46.received), custom_call_target="tpu_custom_call" | custom-call | tf_op jit(solution)/shard_map/finish/pallas_call | solution.py:311
  (5 shorter events, 0.1 us)
Async XLA Ops:
  1.4 5.7 %collective-permute-start = (bf16[2,128,128]{2,1,0:T(8,128)(2,1)S(1)}, bf16[2,128,128]{2,1,0:T(8,128)(2,1)S(1)}, u32[]{:S(2)}, u32[]{:S(2)}) collective-permute-start(bf16[2,128,128]{2,1,0:T(8,128)(2,1)S(1)} %bitcast.18), channel_id=1, source_target_pairs={{0,1},{1,2},{2,3},{3,4},{4,5},{5,6},{6,7},{7,8},{8,9},{9,10},{10,1... | collective-permute-start | bytes 196616 | tf_op jit(solution)/shard_map/ppermute | solution.py:333
  2.8 5.0 %collective-permute-start.1 = (bf16[2,128,128]{2,1,0:T(8,128)(2,1)S(1)}, bf16[2,128,128]{2,1,0:T(8,128)(2,1)S(1)}, u32[]{:S(2)}, u32[]{:S(2)}) collective-permute-start(bf16[2,128,128]{2,1,0:T(8,128)(2,1)S(1)} %bitcast.19), channel_id=1, source_target_pairs={{1,0},{2,1},{3,2},{4,3},{5,4},{6,5},{7,6},{8,7},{9,8},{10,9},{11,1... | collective-permute-start | bytes 196616 | tf_op jit(solution)/shard_map/ppermute | solution.py:333
  4.1 20.7 %copy-start.3 = (bf16[3,3,128,128]{3,2,1,0:T(8,128)(2,1)S(1)}, bf16[3,3,128,128]{3,2,1,0:T(8,128)(2,1)}, u32[]{:S(2)}) copy-start(bf16[3,3,128,128]{3,2,1,0:T(8,128)(2,1)} %weight.3) | copy-start | bytes 884740
  7.8 30.7 %all-to-all-start = ((bf16[4,2048,128]{2,1,0:T(8,128)(2,1)}), bf16[4,2048,128]{2,1,0:T(8,128)(2,1)S(1)}, u32[]{:S(2)}, u32[]{:S(2)}) async-start(bf16[4,2048,128]{2,1,0:T(8,128)(2,1)} %pad_maximum_fusion), calls=%async_computation | async-start | bytes 4194304 | tf_op jit(solution)/shard_map/all_to_all | solution.py:327
  15.5 5.1 %collective-permute-start.2 = (bf16[2,80,128]{2,1,0:T(8,128)(2,1)S(1)}, bf16[2,80,128]{2,1,0:T(8,128)(2,1)S(1)}, u32[]{:S(2)}, u32[]{:S(2)}) collective-permute-start(bf16[2,80,128]{2,1,0:T(8,128)(2,1)S(1)} %fusion.7), channel_id=1, source_target_pairs={{0,16},{16,32},{32,48},{48,64},{64,80},{80,96},{96,112},{1,17},{17... | collective-permute-start | bytes 122888 | tf_op jit(solution)/shard_map/ppermute | solution.py:333
  18.9 5.9 %collective-permute-start.3 = (bf16[2,80,128]{2,1,0:T(8,128)(2,1)S(1)}, bf16[2,80,128]{2,1,0:T(8,128)(2,1)S(1)}, u32[]{:S(2)}, u32[]{:S(2)}) collective-permute-start(bf16[2,80,128]{2,1,0:T(8,128)(2,1)S(1)} %fusion.9), channel_id=1, source_target_pairs={{16,0},{32,16},{48,32},{64,48},{80,64},{96,80},{112,96},{17,1},{33... | collective-permute-start | bytes 122888 | tf_op jit(solution)/shard_map/ppermute | solution.py:333
  38.5 57.1 %copy-start.1 = (bf16[3,2048,128]{2,1,0:T(8,128)(2,1)S(1)}, bf16[3,2048,128]{2,1,0:T(8,128)(2,1)}, u32[]{:S(2)}) copy-start(bf16[3,2048,128]{2,1,0:T(8,128)(2,1)} %weight.4) | copy-start | bytes 4718596
  38.5 27.6 %collective-permute-start.4 = (bf16[4,2048,128]{2,1,0:T(8,128)(2,1)S(1)}, bf16[4,2048,128]{2,1,0:T(8,128)(2,1)S(1)}, u32[]{:S(2)}, u32[]{:S(2)}) collective-permute-start(bf16[4,2048,128]{2,1,0:T(8,128)(2,1)S(1)} %all-to-all-done.own), channel_id=1, source_target_pairs={{0,1},{1,0},{2,3},{3,2},{4,5},{5,4},{6,7},{7,6},{8,9},{9,8},{10,11... | collective-permute-start | bytes 6291464 | tf_op jit(solution)/shard_map/ppermute | solution.py:352
  66.2 39.7 %copy-start.2 = (bf16[128,2048]{1,0:T(8,128)(2,1)S(1)}, bf16[128,2048]{1,0:T(8,128)(2,1)}, u32[]{:S(2)}) copy-start(bf16[128,2048]{1,0:T(8,128)(2,1)} %weight.5) | copy-start | bytes 1572868
  106.5 47.8 %copy-start = (bf16[2,128,4,16,128]{4,3,2,1,0:T(8,128)(2,1)S(1)}, bf16[2,128,4,16,128]{4,3,2,1,0:T(8,128)(2,1)}, u32[]{:S(2)}) copy-start(bf16[2,128,4,16,128]{4,3,2,1,0:T(8,128)(2,1)} %get-tuple-element.19.features) | copy-start | bytes 12582916
where the time goes:
time: 158 us; the launch traced here: 157 us
  blocking collectives  108 us (68%)
  Pallas kernels  19.7 us (12%)
  starting transfers between devices  17.9 us (11%)
  waiting for transfers between devices  6.62 us (4%)
  other arithmetic  3.09 us (2%)
  local copies, waits for them, and re-layouts  2.25 us (1%)
    all_to_all x7, blocking collectives, exchange(): return lax.all_to_all(array, axes, 0, 0, tiled=True)  108 us
    pallas_call x1, Pallas kernels, convolve(): pl.pallas_call(conv_kernel, grid=(2, steps), in_specs=[pl.BlockSpec((1, C...  12.4 us
    all_to_all x1, starting transfers between devices, exchange(): return lax.all_to_all(array, axes, 0, 0, tiled=True)  6.87 us
    ppermute x2, waiting for transfers between devices, from_neighbours(): lax.ppermute(high, axes, backward)  4.92 us
    ppermute x2, starting transfers between devices, from_neighbours(): lax.ppermute(low, axes, forward)  4.69 us
    ppermute x1, starting transfers between devices, on_device(): other = lax.ppermute(own, 'core', [(0, 1), (1, 0)])  3.7 us
  transfers between devices with their start and end apart: 6, of which 4 were waited for; matrix products, arithmetic and copies ran while one was open for 2% of the time, Pallas kernels for 8%

commit v1 on v0

--- a/solution.py
+++ b/solution.py
@@ -14,8 +14,10 @@
 ROW = ("z", "xl")
 COL = ("xh", "y", "core")
 ROWY = ROW + ("y",)
-SAME = ROW + ("xh", "y")
+PLANE = ("xh", "y")
+SAME = ROW + PLANE
 EVERY = ROW + COL
+SWAP = [(0, 1), (1, 0)]
 CHUNK = 64
 SPREAD = 64
 SUB = 16
@@ -31,6 +33,42 @@
 
 
 VMEM = pl.BlockSpec(memory_space=pltpu.VMEM)
+
+
+def pack_kernel(first, second, both, held, arrived, left):
+    pieces = [(i, y, part) for i, part in enumerate((first, second)) for y in range(4)]
+    loads = [
+        pltpu.make_async_copy(part.at[y], held.at[i, y], arrived.at[i, y])
+        for i, y, part in pieces
+    ]
+    stores = [
+        pltpu.make_async_copy(held.at[i, y], both.at[y, pl.ds(1024 * i, 1024)], left.at[i, y])
+        for i, y, _ in pieces
+    ]
+    for copy in loads:
+        copy.start()
+    for load, store in zip(loads, stores):
+        load.wait()
+        store.start()
+    for copy in stores:
+        copy.wait()
+
+
+def pack(first, second):
+    hbm = pl.BlockSpec(memory_space=pltpu.HBM)
+    return pl.pallas_call(
+        pack_kernel,
+        in_specs=[hbm] * 2,
+        out_specs=hbm,
+        out_shape=pltpu.HBM((4, 2048, C), BF),
+        scratch_shapes=[
+            pltpu.VMEM((2, 4, 1024, C), BF),
+            pltpu.SemaphoreType.DMA((2, 4)),
+            pltpu.SemaphoreType.DMA((2, 4)),
+        ],
+        compiler_params=params(),
+        name="pack",
+    )(*(pltpu.with_memory_space_constraint(a, pltpu.HBM) for a in (first, second)))
 
 
 def conv_kernel(
@@ -146,15 +184,14 @@
     )(far, far, far, *near(top, bottom, left, right, weight))
 
 
-def embed_kernel(received, own, other, out, rows, values, wide):
+def embed_kernel(received, own, other, out, rows, values):
     core = lax.axis_index("core")
     rows[...] = received[...].reshape(2048, C).astype(F32)
     for j in range(8):
         values[:, pl.ds(j * C, C)] = rows[pl.ds(j, 256, stride=8), :].astype(BF)
     for which, weight in enumerate((own, other)):
-        for y in range(4):
-            wide[:, pl.ds(y * C, C)] = weight[y, pl.ds(0, 1024)]
-        result = jnp.dot(values[...], wide[...], preferred_element_type=F32).astype(BF)
+        wide = jnp.concatenate([weight[y, pl.ds(0, 1024)] for y in range(4)], axis=1)
+        result = jnp.dot(values[...], wide, preferred_element_type=F32).astype(BF)
         feature = core if which == 0 else 1 - core
         for r in range(8):
             for y in range(4):
@@ -168,7 +205,6 @@
         scratch_shapes=[
             pltpu.VMEM((2048, C), F32),
             pltpu.VMEM((256, 1024), BF),
-            pltpu.VMEM((1024, 512), BF),
         ],
         compiler_params=params(),
         name="embed",
@@ -197,14 +233,10 @@
     )(*near(terms, *base))
 
 
-def qkv_kernel(embedded, weight, queries, pairs):
+def qkv_kernel(own, other, weight, queries, pairs):
     normed = []
-    for core in range(2):
-        blocks = [
-            embedded[pair * 2 + core, feature].astype(F32)
-            for pair in range(8)
-            for feature in range(2)
-        ]
+    for group in (own, other):
+        blocks = [group[pair, feature].astype(F32) for pair in range(8) for feature in range(2)]
         square = sum(block * block for block in blocks)
         square = jnp.sum(square, axis=-1, keepdims=True)
         scale = lax.rsqrt(square * (1.0 / 2048.0) + EPS)
@@ -217,13 +249,13 @@
             pairs[r, part] = result
 
 
-def project_qkv(embedded, weight):
+def project_qkv(own, other, weight):
     return pl.pallas_call(
         qkv_kernel,
         out_shape=[pltpu.VMEM((64, C), BF), pltpu.VMEM((8, 2, 64, C), BF)],
         compiler_params=params(),
         name="qkv",
-    )(*near(embedded, weight))
+    )(*near(own, other, weight))
 
 
 def attend_kernel(queries, pairs, weight, out):
@@ -236,11 +268,13 @@
     weights = (scores / jnp.sum(scores, axis=-1, keepdims=True)).astype(BF)
     attended = jnp.dot(weights, values, preferred_element_type=F32).astype(BF)
     projected = jnp.dot(attended, weight[...], preferred_element_type=F32).astype(BF)
+    core = lax.axis_index("core")
     for pair in range(8):
-        for core in range(2):
+        for which in range(2):
+            target = pair * 2 + (core if which == 0 else 1 - core)
             for feature in range(2):
                 at = (pair * 2 + feature) * C
-                out[pair * 2 + core, feature] = projected[core * 32 : core * 32 + 32, at : at + C]
+                out[target, feature] = projected[which * 32 : which * 32 + 32, at : at + C]
 
 
 def attend(queries, pairs, weight):
@@ -252,22 +286,26 @@
     )(*near(queries, pairs, weight))
 
 
-def unembed_kernel(mixed, own, other, out, values, wide, rows):
+def unembed_kernel(mixed, own, other, out, values, rows):
     core = lax.axis_index("core")
-    for which, weight in enumerate((own, other)):
+    for which in range(2):
         feature = core if which == 0 else 1 - core
         for y in range(4):
-            at = pl.ds((which * 4 + y) * C, C)
-            wide[:, at] = weight[y, pl.ds(1024, 1024)]
             for r in range(8):
+                at = pl.ds((which * 4 + y) * C, C)
                 values[pl.ds(r * 32, 32), at] = mixed[r * 4 + y, feature]
-    for j in range(8):
-        rows[pl.ds(j, 256, stride=8), :] = lax.dot_general(
+    for pair in range(4):
+        at = pl.ds(1024 + pair * 2 * C, 2 * C)
+        wide = [weight[y, at] for weight in (own, other) for y in range(4)]
+        result = lax.dot_general(
             values[...],
-            wide[pl.ds(j * C, C), :],
+            jnp.concatenate(wide, axis=1),
             (((1,), (1,)), ((), ())),
             preferred_element_type=F32,
         )
+        for j in range(2):
+            column = result[:, j * C : j * C + C]
+            rows[pl.ds(2 * pair + j, 256, stride=8), :] = column
     out[...] = rows[...].astype(BF).reshape(64, 32, C)
 
 
@@ -277,7 +315,6 @@
         out_shape=pltpu.VMEM((64, 32, C), BF),
         scratch_shapes=[
             pltpu.VMEM((256, 1024), BF),
-            pltpu.VMEM((1024, 1024), BF),
             pltpu.VMEM((2048, C), F32),
         ],
         compiler_params=params(),
@@ -335,8 +372,8 @@
 
 def on_device(frames, conv_weight, embed_weight, unembed_weight, qkv_weight, out_weight):
     left, right = from_neighbours(frames[:, :, 63], frames[:, :, 0], COL, 16)
-    both = [weight.reshape(4, 1024, C) for weight in (embed_weight, unembed_weight)]
-    both = jnp.concatenate(both, axis=1)
+    maps = [weight.reshape(4, 1024, C) for weight in (embed_weight, unembed_weight)]
+    both = pack(*maps)
     left, right, both = lax.optimization_barrier((left, right, both))
     rows = [
         jnp.pad(
@@ -349,10 +386,11 @@
     own = exchange(both, "y")
     features, patches = convolve(frames, top, bottom, left, right, conv_weight)
     own, patches = lax.optimization_barrier((own, patches))
-    other = lax.ppermute(own, "core", [(0, 1), (1, 0)])
+    other = lax.ppermute(own, "core", SWAP)
     partial = embed(exchange(patches, SAME), own, other)
-    copies, embedded = sum_and_copy(16, exchange(partial, ROWY))
-    queries, pairs = project_qkv(exchange(copies, COL), qkv_weight)
+    copies, embedded = sum_and_copy(8, exchange(partial, ROWY))
+    group = exchange(copies, PLANE)
+    queries, pairs = project_qkv(group, lax.ppermute(group, "core", SWAP), qkv_weight)
     projected = attend(queries, exchange(pairs, ROW), out_weight)
     copies, _ = sum_and_copy(32, exchange(projected, COL), embedded)
     patch_values = unembed(exchange(copies, ROWY), own, other)

time: 158 us -> 156 us (0.987)
  other arithmetic: 3.09 us -> 0.02 us
  blocking collectives: 108 us -> 106 us
  Pallas kernels: 19.7 us -> 21.3 us
    concatenate x1 -> x0, other arithmetic: 3.07 us -> none  [on_device(): both = jnp.concatenate(both, axis=1)]
    pallas_call x0 -> x1, Pallas kernels: none -> 2.47 us  [pack(): pl.pallas_call(pack_kernel, in_specs=[hbm] * 2, out_specs=hbm, out_shape=...]
    ppermute x1 -> x2, starting transfers between devices: 3.7 us -> 4.28 us  [the longest x1 4.28 us: on_device(): other = lax.ppermute(own, 'core', SWAP)]
  transfers between devices with their start and end apart: 6 -> 7, of which waited for: 4 -> 5; matrix products, arithmetic and copies ran while one was open for 2% -> 1% of each run, Pallas kernels for 8% -> 10%
where the time goes in v1:
time: 156 us
  blocking collectives  106 us (68%)
  Pallas kernels  21.3 us (14%)
  starting transfers between devices  17.9 us (11%)
  waiting for transfers between devices  7.97 us (5%)
  local copies, waits for them, and re-layouts  2.25 us (1%)
    all_to_all x7, blocking collectives, exchange(): return lax.all_to_all(array, axes, 0, 0, tiled=True)  106 us
    pallas_call x1, Pallas kernels, convolve(): pl.pallas_call(conv_kernel, grid=(2, steps), in_specs=[pl.BlockSpec((1, C...  12.4 us
    all_to_all x1, starting transfers between devices, exchange(): return lax.all_to_all(array, axes, 0, 0, tiled=True)  6.3 us
    ppermute x2, waiting for transfers between devices, from_neighbours(): lax.ppermute(high, axes, backward)  5.5 us
    ppermute x2, starting transfers between devices, from_neighbours(): lax.ppermute(low, axes, forward)  4.69 us
    ppermute x1, starting transfers between devices, on_device(): other = lax.ppermute(own, 'core', SWAP)  4.28 us
  transfers between devices with their start and end apart: 7, of which 5 were waited for; matrix products, arithmetic and copies ran while one was open for 1% of the time, Pallas kernels for 10%

profile of v1, /device:TPU:0, one launch (start us, length us, event | category | flops | bytes accessed | tf_op | source)
XLA Modules:
  0.0 155.8 jit_solution(1124083697389611098)
XLA Ops:
  0.0 1.4 fusion.10
  1.4 1.3 collective-permute-start
  2.8 1.3 collective-permute-start.1
  4.1 0.0 copy-start.3
  4.1 2.5 %pack.1 = bf16[4,2048,128]{2,1,0:T(8,128)(2,1)} custom-call(bf16[4,1024,128]{2,1,0:T(8,128)(2,1)} %bitcast.16, bf16[4,1024,128]{2,1,0:T(8,128)(2,1)} %bitcast.17), custom_call_target="tpu_custom_call" | custom-call | tf_op jit(solution)/shard_map/pack/pallas_call | solution.py:59
  6.6 0.0 collective-permute-done.left
  6.6 1.2 collective-permute-done.1.right
  7.8 6.3 %all-to-all-start = ((bf16[4,2048,128]{2,1,0:T(8,128)(2,1)}), bf16[4,2048,128]{2,1,0:T(8,128)(2,1)S(1)}, u32[]{:S(2)}, u32[]{:S(2)}) async-start(bf16[4,2048,128]{2,1,0:T(8,128)(2,1)} %pack.1), calls=%async_computation | async-start | bytes 4194304 | tf_op jit(solution)/shard_map/all_to_all | solution.py:364
  14.1 0.8 slice_bitcast_fusion
  14.9 3.4 %collective-permute-start.2 = (bf16[2,80,128]{2,1,0:T(8,128)(2,1)S(1)}, bf16[2,80,128]{2,1,0:T(8,128)(2,1)S(1)}, u32[]{:S(2)}, u32[]{:S(2)}) collective-permute-start(bf16[2,80,128]{2,1,0:T(8,128)(2,1)S(1)} %fusion.7), channel_id=1, source_target_pairs={{0,16},{16,32},{32,48},{48,64},{64,80},{80,96},{96,112},{1,17},{17... | collective-permute-start | bytes 122888 | tf_op jit(solution)/shard_map/ppermute | solution.py:370
  18.3 1.3 collective-permute-start.3
  19.6 0.3 collective-permute-done.2.top
  20.0 4.3 %collective-permute-done.3.bottom = bf16[2,80,128]{2,1,0:T(8,128)(2,1)S(1)} collective-permute-done((bf16[2,80,128]{2,1,0:T(8,128)(2,1)S(1)}, bf16[2,80,128]{2,1,0:T(8,128)(2,1)S(1)}, u32[]{:S(2)}, u32[]{:S(2)}) %collective-permute-start.3) | collective-permute-done | bytes 40992 | tf_op jit(solution)/shard_map/ppermute | solution.py:370
  24.2 0.0 copy-done.3
  24.2 12.4 %conv_block.1 = (bf16[2,128,4,16,128]{4,3,2,1,0:T(8,128)(2,1)}, bf16[64,32,128]{2,1,0:T(8,128)(2,1)S(1)}) custom-call(bf16[2,128,64,128]{3,2,1,0:T(8,128)(2,1)} %below.1, bf16[2,128,64,128]{3,2,1,0:T(8,128)(2,1)} %below.1, bf16[2,128,64,128]{3,2,1,0:T(8,128)(2,1)} %below.1, bf16[2,80,128]{2,1,0:T(8,128)(2,1)S(1)} %collective-permute-done.2.top, ...), custom_call_target="tpu_custom_call" | custom-call | flops 4831838208 | bytes 9437184 | tf_op jit(solution)/shard_map/conv_block/pallas_call | solution.py:159
  36.6 0.8 all-to-all-done.own
  37.4 0.0 copy-start.1
  37.4 4.3 %collective-permute-start.4 = (bf16[4,2048,128]{2,1,0:T(8,128)(2,1)S(1)}, bf16[4,2048,128]{2,1,0:T(8,128)(2,1)S(1)}, u32[]{:S(2)}, u32[]{:S(2)}) collective-permute-start(bf16[4,2048,128]{2,1,0:T(8,128)(2,1)S(1)} %all-to-all-done.own), channel_id=1, source_target_pairs={{0,1},{1,0},{2,3},{3,2},{4,5},{5,4},{6,7},{7,6},{8,9},{9,8},{10,11... | collective-permute-start | bytes 6291464 | tf_op jit(solution)/shard_map/ppermute | solution.py:389
  41.7 23.9 %all_to_all.40.received = bf16[64,32,128]{2,1,0:T(8,128)(2,1)S(1)} all-to-all(bf16[64,32,128]{2,1,0:T(8,128)(2,1)S(1)} %get-tuple-element.22), channel_id=1, replica_groups=mesh['z'=4,'xl'=2,'xh'=2,'y'=4,'core'=2] {'z','xl','xh','y'}, dimensions={0} | all-to-all | bytes 1048576 | tf_op jit(solution)/shard_map/all_to_all | solution.py:364
  65.6 0.0 copy-start.2
  65.6 0.0 collective-permute-done.4.other
  65.6 0.8 embed.1
  66.5 14.0 %all_to_all.41.terms = bf16[32,2,32,128]{3,2,1,0:T(8,128)(2,1)S(1)} all-to-all(bf16[32,2,32,128]{3,2,1,0:T(8,128)(2,1)S(1)} %embed.1), channel_id=1, replica_groups=mesh['z'=4,'xl'=2,'xh'=2,'y'=4,'core'=2] {'z','xl','y'}, dimensions={0} | all-to-all | bytes 1048576 | tf_op jit(solution)/shard_map/all_to_all | solution.py:364
  80.5 0.1 sum_and_copy.2
  80.6 12.6 %all_to_all.42.own = bf16[8,2,32,128]{3,2,1,0:T(8,128)(2,1)S(1)} all-to-all(bf16[8,2,32,128]{3,2,1,0:T(8,128)(2,1)S(1)} %get-tuple-element.24), channel_id=1, replica_groups=mesh['z'=4,'xl'=2,'xh'=2,'y'=4,'core'=2] {'xh','y'}, dimensions={0} | all-to-all | bytes 262144 | tf_op jit(solution)/shard_map/all_to_all | solution.py:364
  93.2 0.0 collective-permute-start.5
  93.2 1.3 collective-permute-done.5.other
  94.5 0.0 copy-done.1
  94.5 0.5 qkv.1
  95.0 10.3 %all_to_all.43.pairs = bf16[8,2,64,128]{3,2,1,0:T(8,128)(2,1)S(1)} all-to-all(bf16[8,2,64,128]{3,2,1,0:T(8,128)(2,1)S(1)} %get-tuple-element.26), channel_id=1, replica_groups=mesh['z'=4,'xl'=2,'xh'=2,'y'=4,'core'=2] {'z','xl'}, dimensions={0} | all-to-all | bytes 524288 | tf_op jit(solution)/shard_map/all_to_all | solution.py:364
  105.3 0.0 copy-done.2
  105.3 0.7 attend.1
  106.0 0.0 copy-start
  106.0 12.5 %all_to_all.44.terms = bf16[16,2,32,128]{3,2,1,0:T(8,128)(2,1)S(1)} all-to-all(bf16[16,2,32,128]{3,2,1,0:T(8,128)(2,1)S(1)} %attend.1), channel_id=1, replica_groups=mesh['z'=4,'xl'=2,'xh'=2,'y'=4,'core'=2] {'xh','y','core'}, dimensions={0} | all-to-all | bytes 524288 | tf_op jit(solution)/shard_map/all_to_all | solution.py:364
  118.4 0.7 sum_and_copy.3
  119.1 15.0 %all_to_all.45.mixed = bf16[32,2,32,128]{3,2,1,0:T(8,128)(2,1)S(1)} all-to-all(bf16[32,2,32,128]{3,2,1,0:T(8,128)(2,1)S(1)} %get-tuple-element.28), channel_id=1, replica_groups=mesh['z'=4,'xl'=2,'xh'=2,'y'=4,'core'=2] {'z','xl','y'}, dimensions={0} | all-to-all | bytes 1048576 | tf_op jit(solution)/shard_map/all_to_all | solution.py:364
  134.1 0.8 unembed.1
  135.0 17.9 %all_to_all.46.received = bf16[64,32,128]{2,1,0:T(8,128)(2,1)S(1)} all-to-all(bf16[64,32,128]{2,1,0:T(8,128)(2,1)S(1)} %unembed.1), channel_id=1, replica_groups=mesh['z'=4,'xl'=2,'xh'=2,'y'=4,'core'=2] {'z','xl','xh','y'}, dimensions={0} | all-to-all | bytes 1048576 | tf_op jit(solution)/shard_map/all_to_all | solution.py:364
  152.9 0.0 copy-done
  152.9 2.8 %finish.1 = bf16[2,128,64,128]{3,2,1,0:T(8,128)(2,1)} custom-call(bf16[2,128,4,16,128]{4,3,2,1,0:T(8,128)(2,1)S(1)} %copy-done, bf16[64,32,128]{2,1,0:T(8,128)(2,1)S(1)} %all_to_all.46.received), custom_call_target="tpu_custom_call" | custom-call | tf_op jit(solution)/shard_map/finish/pallas_call | solution.py:348
  (5 shorter events, 0.1 us)
Async XLA Ops:
  1.4 5.1 %collective-permute-start = (bf16[2,128,128]{2,1,0:T(8,128)(2,1)S(1)}, bf16[2,128,128]{2,1,0:T(8,128)(2,1)S(1)}, u32[]{:S(2)}, u32[]{:S(2)}) collective-permute-start(bf16[2,128,128]{2,1,0:T(8,128)(2,1)S(1)} %bitcast.18), channel_id=1, source_target_pairs={{0,1},{1,2},{2,3},{3,4},{4,5},{5,6},{6,7},{7,8},{8,9},{9,10},{10,1... | collective-permute-start | bytes 196616 | tf_op jit(solution)/shard_map/ppermute | solution.py:370
  2.8 5.0 %collective-permute-start.1 = (bf16[2,128,128]{2,1,0:T(8,128)(2,1)S(1)}, bf16[2,128,128]{2,1,0:T(8,128)(2,1)S(1)}, u32[]{:S(2)}, u32[]{:S(2)}) collective-permute-start(bf16[2,128,128]{2,1,0:T(8,128)(2,1)S(1)} %bitcast.19), channel_id=1, source_target_pairs={{1,0},{2,1},{3,2},{4,3},{5,4},{6,5},{7,6},{8,7},{9,8},{10,9},{11,1... | collective-permute-start | bytes 196616 | tf_op jit(solution)/shard_map/ppermute | solution.py:370
  4.1 20.2 %copy-start.3 = (bf16[3,3,128,128]{3,2,1,0:T(8,128)(2,1)S(1)}, bf16[3,3,128,128]{3,2,1,0:T(8,128)(2,1)}, u32[]{:S(2)}) copy-start(bf16[3,3,128,128]{3,2,1,0:T(8,128)(2,1)} %weight.3) | copy-start | bytes 884740
  7.8 29.6 %all-to-all-start = ((bf16[4,2048,128]{2,1,0:T(8,128)(2,1)}), bf16[4,2048,128]{2,1,0:T(8,128)(2,1)S(1)}, u32[]{:S(2)}, u32[]{:S(2)}) async-start(bf16[4,2048,128]{2,1,0:T(8,128)(2,1)} %pack.1), calls=%async_computation | async-start | bytes 4194304 | tf_op jit(solution)/shard_map/all_to_all | solution.py:364
  14.9 5.1 %collective-permute-start.2 = (bf16[2,80,128]{2,1,0:T(8,128)(2,1)S(1)}, bf16[2,80,128]{2,1,0:T(8,128)(2,1)S(1)}, u32[]{:S(2)}, u32[]{:S(2)}) collective-permute-start(bf16[2,80,128]{2,1,0:T(8,128)(2,1)S(1)} %fusion.7), channel_id=1, source_target_pairs={{0,16},{16,32},{32,48},{48,64},{64,80},{80,96},{96,112},{1,17},{17... | collective-permute-start | bytes 122888 | tf_op jit(solution)/shard_map/ppermute | solution.py:370
  18.3 5.9 %collective-permute-start.3 = (bf16[2,80,128]{2,1,0:T(8,128)(2,1)S(1)}, bf16[2,80,128]{2,1,0:T(8,128)(2,1)S(1)}, u32[]{:S(2)}, u32[]{:S(2)}) collective-permute-start(bf16[2,80,128]{2,1,0:T(8,128)(2,1)S(1)} %fusion.9), channel_id=1, source_target_pairs={{16,0},{32,16},{48,32},{64,48},{80,64},{96,80},{112,96},{17,1},{33... | collective-permute-start | bytes 122888 | tf_op jit(solution)/shard_map/ppermute | solution.py:370
  37.4 57.1 %copy-start.1 = (bf16[3,2048,128]{2,1,0:T(8,128)(2,1)S(1)}, bf16[3,2048,128]{2,1,0:T(8,128)(2,1)}, u32[]{:S(2)}) copy-start(bf16[3,2048,128]{2,1,0:T(8,128)(2,1)} %weight.4) | copy-start | bytes 4718596
  37.4 28.2 %collective-permute-start.4 = (bf16[4,2048,128]{2,1,0:T(8,128)(2,1)S(1)}, bf16[4,2048,128]{2,1,0:T(8,128)(2,1)S(1)}, u32[]{:S(2)}, u32[]{:S(2)}) collective-permute-start(bf16[4,2048,128]{2,1,0:T(8,128)(2,1)S(1)} %all-to-all-done.own), channel_id=1, source_target_pairs={{0,1},{1,0},{2,3},{3,2},{4,5},{5,4},{6,7},{7,6},{8,9},{9,8},{10,11... | collective-permute-start | bytes 6291464 | tf_op jit(solution)/shard_map/ppermute | solution.py:389
  65.6 39.7 %copy-start.2 = (bf16[128,2048]{1,0:T(8,128)(2,1)S(1)}, bf16[128,2048]{1,0:T(8,128)(2,1)}, u32[]{:S(2)}) copy-start(bf16[128,2048]{1,0:T(8,128)(2,1)} %weight.5) | copy-start | bytes 1572868
  93.2 1.3 collective-permute-start.5
  106.0 47.0 %copy-start = (bf16[2,128,4,16,128]{4,3,2,1,0:T(8,128)(2,1)S(1)}, bf16[2,128,4,16,128]{4,3,2,1,0:T(8,128)(2,1)}, u32[]{:S(2)}) copy-start(bf16[2,128,4,16,128]{4,3,2,1,0:T(8,128)(2,1)} %get-tuple-element.19.features) | copy-start | bytes 12582916

commit v2 on v1

--- a/solution.py
+++ b/solution.py
@@ -13,19 +13,27 @@
 EPS = 1e-06
 ROW = ("z", "xl")
 COL = ("xh", "y", "core")
-ROWY = ROW + ("y",)
+ROWY = ("xl", "y", "z")
 PLANE = ("xh", "y")
-SAME = ROW + PLANE
+SAME = ("y", "xh", "xl", "z")
 EVERY = ROW + COL
 SWAP = [(0, 1), (1, 0)]
 CHUNK = 64
-SPREAD = 64
+SPREAD = 128
 SUB = 16
 LEFT = 8
 
 
 def params(mib=12):
     return pltpu.CompilerParams(vmem_limit_bytes=mib * 2**20)
+
+
+def in_rowy(r, y):
+    return ((r % 2) * 4 + y) * 4 + r // 2
+
+
+def in_same(r, xh, y):
+    return ((y * 2 + xh) * 2 + r % 2) * 4 + r // 2
 
 
 def near(*arrays):
@@ -150,7 +158,7 @@
             for y in range(4):
                 block = pooled[r * 4 + y].astype(BF)
                 for xh in range(2):
-                    send[(r * 2 + xh) * 4 + y] = block
+                    send[in_same(r, xh, y)] = block
 
 
 def convolve(frames, top, bottom, left, right, weight):
@@ -186,7 +194,11 @@
 
 def embed_kernel(received, own, other, out, rows, values):
     core = lax.axis_index("core")
-    rows[...] = received[...].reshape(2048, C).astype(F32)
+    for r in range(8):
+        for xh in range(2):
+            for y in range(4):
+                at = pl.ds(((r * 2 + xh) * 4 + y) * 32, 32)
+                rows[at, :] = received[in_same(r, xh, y)].astype(F32)
     for j in range(8):
         values[:, pl.ds(j * C, C)] = rows[pl.ds(j, 256, stride=8), :].astype(BF)
     for which, weight in enumerate((own, other)):
@@ -195,7 +207,7 @@
         feature = core if which == 0 else 1 - core
         for r in range(8):
             for y in range(4):
-                out[r * 4 + y, feature] = result[r * 32 : r * 32 + 32, y * C : y * C + C]
+                out[in_rowy(r, y), feature] = result[r * 32 : r * 32 + 32, y * C : y * C + C]
 
 
 def embed(received, own, other):
@@ -293,7 +305,7 @@
         for y in range(4):
             for r in range(8):
                 at = pl.ds((which * 4 + y) * C, C)
-                values[pl.ds(r * 32, 32), at] = mixed[r * 4 + y, feature]
+                values[pl.ds(r * 32, 32), at] = mixed[in_rowy(r, y), feature]
     for pair in range(4):
         at = pl.ds(1024 + pair * 2 * C, 2 * C)
         wide = [weight[y, at] for weight in (own, other) for y in range(4)]
@@ -306,7 +318,11 @@
         for j in range(2):
             column = result[:, j * C : j * C + C]
             rows[pl.ds(2 * pair + j, 256, stride=8), :] = column
-    out[...] = rows[...].astype(BF).reshape(64, 32, C)
+    for r in range(8):
+        for xh in range(2):
+            for y in range(4):
+                at = pl.ds(((r * 2 + xh) * 4 + y) * 32, 32)
+                out[in_same(r, xh, y)] = rows[at, :].astype(BF)
 
 
 def unembed(mixed, own, other):
@@ -329,13 +345,14 @@
     def _():
         for r in range(8):
             for y in range(4):
-                total = received[r * 8 + y].astype(F32) + received[r * 8 + 4 + y].astype(F32)
+                first, second = (received[in_same(r, xh, y)].astype(F32) for xh in range(2))
+                total = first + second
                 patch[r * 4 + y] = total.astype(BF).astype(F32)
 
-    token = frame * 2 + step
-    at = pl.ds(pl.multiple_of(token * 8, 8), 8)
     for q in range(SPREAD // 4):
-        piece = q * 2
+        token = frame * 2 + q // 16
+        at = pl.ds(pl.multiple_of(token * 8, 8), 8)
+        piece = q % 16 * 2
         small = jnp.concatenate([patch[piece, at, :], patch[piece + 1, at, :]], axis=0)
         for row in range(4):
             for m in range(4):

time: 156 us -> 155 us (level)
  no operation moved by 1% of the time
where the time goes in v2:
time: 155 us
  blocking collectives  106 us (68%)
  Pallas kernels  21 us (14%)
  starting transfers between devices  17.9 us (12%)
  waiting for transfers between devices  7.97 us (5%)
  local copies, waits for them, and re-layouts  2.25 us (1%)
    all_to_all x7, blocking collectives, exchange(): return lax.all_to_all(array, axes, 0, 0, tiled=True)  106 us
    pallas_call x1, Pallas kernels, convolve(): pl.pallas_call(conv_kernel, grid=(2, steps), in_specs=[pl.BlockSpec((1, C...  12.4 us
    all_to_all x1, starting transfers between devices, exchange(): return lax.all_to_all(array, axes, 0, 0, tiled=True)  6.3 us
    ppermute x2, waiting for transfers between devices, from_neighbours(): lax.ppermute(high, axes, backward)  5.5 us
    ppermute x2, starting transfers between devices, from_neighbours(): lax.ppermute(low, axes, forward)  4.69 us
    ppermute x1, starting transfers between devices, on_device(): other = lax.ppermute(own, 'core', SWAP)  4.28 us
  transfers between devices with their start and end apart: 7, of which 5 were waited for; matrix products, arithmetic and copies ran while one was open for 1% of the time, Pallas kernels for 10%

profile of v2, /device:TPU:0, one launch (start us, length us, event | category | flops | bytes accessed | tf_op | source)
XLA Modules:
  0.0 154.8 jit_solution(9705851441087056618)
XLA Ops:
  0.0 1.4 fusion.10
  1.4 1.3 collective-permute-start
  2.8 1.3 collective-permute-start.1
  4.1 0.0 copy-start.3
  4.1 2.5 %pack.1 = bf16[4,2048,128]{2,1,0:T(8,128)(2,1)} custom-call(bf16[4,1024,128]{2,1,0:T(8,128)(2,1)} %bitcast.16, bf16[4,1024,128]{2,1,0:T(8,128)(2,1)} %bitcast.17), custom_call_target="tpu_custom_call" | custom-call | tf_op jit(solution)/shard_map/pack/pallas_call | solution.py:67
  6.6 0.0 collective-permute-done.left
  6.6 1.2 collective-permute-done.1.right
  7.8 6.3 %all-to-all-start = ((bf16[4,2048,128]{2,1,0:T(8,128)(2,1)}), bf16[4,2048,128]{2,1,0:T(8,128)(2,1)S(1)}, u32[]{:S(2)}, u32[]{:S(2)}) async-start(bf16[4,2048,128]{2,1,0:T(8,128)(2,1)} %pack.1), calls=%async_computation | async-start | bytes 4194304 | tf_op jit(solution)/shard_map/all_to_all | solution.py:381
  14.1 0.8 slice_bitcast_fusion
  14.9 3.4 %collective-permute-start.2 = (bf16[2,80,128]{2,1,0:T(8,128)(2,1)S(1)}, bf16[2,80,128]{2,1,0:T(8,128)(2,1)S(1)}, u32[]{:S(2)}, u32[]{:S(2)}) collective-permute-start(bf16[2,80,128]{2,1,0:T(8,128)(2,1)S(1)} %fusion.7), channel_id=1, source_target_pairs={{0,16},{16,32},{32,48},{48,64},{64,80},{80,96},{96,112},{1,17},{17... | collective-permute-start | bytes 122888 | tf_op jit(solution)/shard_map/ppermute | solution.py:387
  18.3 1.3 collective-permute-start.3
  19.6 0.3 collective-permute-done.2.top
  20.0 4.3 %collective-permute-done.3.bottom = bf16[2,80,128]{2,1,0:T(8,128)(2,1)S(1)} collective-permute-done((bf16[2,80,128]{2,1,0:T(8,128)(2,1)S(1)}, bf16[2,80,128]{2,1,0:T(8,128)(2,1)S(1)}, u32[]{:S(2)}, u32[]{:S(2)}) %collective-permute-start.3) | collective-permute-done | bytes 40992 | tf_op jit(solution)/shard_map/ppermute | solution.py:387
  24.2 0.0 copy-done.3
  24.2 12.4 %conv_block.1 = (bf16[2,128,4,16,128]{4,3,2,1,0:T(8,128)(2,1)}, bf16[64,32,128]{2,1,0:T(8,128)(2,1)S(1)}) custom-call(bf16[2,128,64,128]{3,2,1,0:T(8,128)(2,1)} %below.1, bf16[2,128,64,128]{3,2,1,0:T(8,128)(2,1)} %below.1, bf16[2,128,64,128]{3,2,1,0:T(8,128)(2,1)} %below.1, bf16[2,80,128]{2,1,0:T(8,128)(2,1)S(1)} %collective-permute-done.2.top, ...), custom_call_target="tpu_custom_call" | custom-call | flops 4831838208 | bytes 9437184 | tf_op jit(solution)/shard_map/conv_block/pallas_call | solution.py:167
  36.6 0.8 all-to-all-done.own
  37.4 0.0 copy-start.1
  37.4 4.3 %collective-permute-start.4 = (bf16[4,2048,128]{2,1,0:T(8,128)(2,1)S(1)}, bf16[4,2048,128]{2,1,0:T(8,128)(2,1)S(1)}, u32[]{:S(2)}, u32[]{:S(2)}) collective-permute-start(bf16[4,2048,128]{2,1,0:T(8,128)(2,1)S(1)} %all-to-all-done.own), channel_id=1, source_target_pairs={{0,1},{1,0},{2,3},{3,2},{4,5},{5,4},{6,7},{7,6},{8,9},{9,8},{10,11... | collective-permute-start | bytes 6291464 | tf_op jit(solution)/shard_map/ppermute | solution.py:406
  41.7 24.1 %all_to_all.40.received = bf16[64,32,128]{2,1,0:T(8,128)(2,1)S(1)} all-to-all(bf16[64,32,128]{2,1,0:T(8,128)(2,1)S(1)} %get-tuple-element.22), channel_id=1, replica_groups=mesh['z'=4,'xl'=2,'xh'=2,'y'=4,'core'=2] {'y','xh','xl','z'}, dimensions={0} | all-to-all | bytes 1048576 | tf_op jit(solution)/shard_map/all_to_all | solution.py:381
  65.8 0.0 copy-start.2
  65.8 0.0 collective-permute-done.4.other
  65.8 0.8 embed.1
  66.6 13.7 %all_to_all.41.terms = bf16[32,2,32,128]{3,2,1,0:T(8,128)(2,1)S(1)} all-to-all(bf16[32,2,32,128]{3,2,1,0:T(8,128)(2,1)S(1)} %embed.1), channel_id=1, replica_groups=mesh['z'=4,'xl'=2,'xh'=2,'y'=4,'core'=2] {'xl','y','z'}, dimensions={0} | all-to-all | bytes 1048576 | tf_op jit(solution)/shard_map/all_to_all | solution.py:381
  80.3 0.1 sum_and_copy.2
  80.4 12.6 %all_to_all.42.own = bf16[8,2,32,128]{3,2,1,0:T(8,128)(2,1)S(1)} all-to-all(bf16[8,2,32,128]{3,2,1,0:T(8,128)(2,1)S(1)} %get-tuple-element.24), channel_id=1, replica_groups=mesh['z'=4,'xl'=2,'xh'=2,'y'=4,'core'=2] {'xh','y'}, dimensions={0} | all-to-all | bytes 262144 | tf_op jit(solution)/shard_map/all_to_all | solution.py:381
  93.0 0.0 collective-permute-start.5
  93.0 1.3 collective-permute-done.5.other
  94.4 0.0 copy-done.1
  94.4 0.5 qkv.1
  94.9 10.3 %all_to_all.43.pairs = bf16[8,2,64,128]{3,2,1,0:T(8,128)(2,1)S(1)} all-to-all(bf16[8,2,64,128]{3,2,1,0:T(8,128)(2,1)S(1)} %get-tuple-element.26), channel_id=1, replica_groups=mesh['z'=4,'xl'=2,'xh'=2,'y'=4,'core'=2] {'z','xl'}, dimensions={0} | all-to-all | bytes 524288 | tf_op jit(solution)/shard_map/all_to_all | solution.py:381
  105.1 0.0 copy-done.2
  105.2 0.7 attend.1
  105.8 0.0 copy-start
  105.8 12.5 %all_to_all.44.terms = bf16[16,2,32,128]{3,2,1,0:T(8,128)(2,1)S(1)} all-to-all(bf16[16,2,32,128]{3,2,1,0:T(8,128)(2,1)S(1)} %attend.1), channel_id=1, replica_groups=mesh['z'=4,'xl'=2,'xh'=2,'y'=4,'core'=2] {'xh','y','core'}, dimensions={0} | all-to-all | bytes 524288 | tf_op jit(solution)/shard_map/all_to_all | solution.py:381
  118.3 0.7 sum_and_copy.3
  119.0 15.2 %all_to_all.45.mixed = bf16[32,2,32,128]{3,2,1,0:T(8,128)(2,1)S(1)} all-to-all(bf16[32,2,32,128]{3,2,1,0:T(8,128)(2,1)S(1)} %get-tuple-element.28), channel_id=1, replica_groups=mesh['z'=4,'xl'=2,'xh'=2,'y'=4,'core'=2] {'xl','y','z'}, dimensions={0} | all-to-all | bytes 1048576 | tf_op jit(solution)/shard_map/all_to_all | solution.py:381
  134.2 0.8 unembed.1
  135.0 17.2 %all_to_all.46.received = bf16[64,32,128]{2,1,0:T(8,128)(2,1)S(1)} all-to-all(bf16[64,32,128]{2,1,0:T(8,128)(2,1)S(1)} %unembed.1), channel_id=1, replica_groups=mesh['z'=4,'xl'=2,'xh'=2,'y'=4,'core'=2] {'y','xh','xl','z'}, dimensions={0} | all-to-all | bytes 1048576 | tf_op jit(solution)/shard_map/all_to_all | solution.py:381
  152.2 0.0 copy-done
  152.2 2.6 %finish.1 = bf16[2,128,64,128]{3,2,1,0:T(8,128)(2,1)} custom-call(bf16[2,128,4,16,128]{4,3,2,1,0:T(8,128)(2,1)S(1)} %copy-done, bf16[64,32,128]{2,1,0:T(8,128)(2,1)S(1)} %all_to_all.46.received), custom_call_target="tpu_custom_call" | custom-call | tf_op jit(solution)/shard_map/finish/pallas_call | solution.py:365
  (5 shorter events, 0.1 us)
Async XLA Ops:
  1.4 5.1 %collective-permute-start = (bf16[2,128,128]{2,1,0:T(8,128)(2,1)S(1)}, bf16[2,128,128]{2,1,0:T(8,128)(2,1)S(1)}, u32[]{:S(2)}, u32[]{:S(2)}) collective-permute-start(bf16[2,128,128]{2,1,0:T(8,128)(2,1)S(1)} %bitcast.18), channel_id=1, source_target_pairs={{0,1},{1,2},{2,3},{3,4},{4,5},{5,6},{6,7},{7,8},{8,9},{9,10},{10,1... | collective-permute-start | bytes 196616 | tf_op jit(solution)/shard_map/ppermute | solution.py:387
  2.8 5.0 %collective-permute-start.1 = (bf16[2,128,128]{2,1,0:T(8,128)(2,1)S(1)}, bf16[2,128,128]{2,1,0:T(8,128)(2,1)S(1)}, u32[]{:S(2)}, u32[]{:S(2)}) collective-permute-start(bf16[2,128,128]{2,1,0:T(8,128)(2,1)S(1)} %bitcast.19), channel_id=1, source_target_pairs={{1,0},{2,1},{3,2},{4,3},{5,4},{6,5},{7,6},{8,7},{9,8},{10,9},{11,1... | collective-permute-start | bytes 196616 | tf_op jit(solution)/shard_map/ppermute | solution.py:387
  4.1 20.2 %copy-start.3 = (bf16[3,3,128,128]{3,2,1,0:T(8,128)(2,1)S(1)}, bf16[3,3,128,128]{3,2,1,0:T(8,128)(2,1)}, u32[]{:S(2)}) copy-start(bf16[3,3,128,128]{3,2,1,0:T(8,128)(2,1)} %weight.3) | copy-start | bytes 884740
  7.8 29.6 %all-to-all-start = ((bf16[4,2048,128]{2,1,0:T(8,128)(2,1)}), bf16[4,2048,128]{2,1,0:T(8,128)(2,1)S(1)}, u32[]{:S(2)}, u32[]{:S(2)}) async-start(bf16[4,2048,128]{2,1,0:T(8,128)(2,1)} %pack.1), calls=%async_computation | async-start | bytes 4194304 | tf_op jit(solution)/shard_map/all_to_all | solution.py:381
  14.9 5.1 %collective-permute-start.2 = (bf16[2,80,128]{2,1,0:T(8,128)(2,1)S(1)}, bf16[2,80,128]{2,1,0:T(8,128)(2,1)S(1)}, u32[]{:S(2)}, u32[]{:S(2)}) collective-permute-start(bf16[2,80,128]{2,1,0:T(8,128)(2,1)S(1)} %fusion.7), channel_id=1, source_target_pairs={{0,16},{16,32},{32,48},{48,64},{64,80},{80,96},{96,112},{1,17},{17... | collective-permute-start | bytes 122888 | tf_op jit(solution)/shard_map/ppermute | solution.py:387
  18.3 5.9 %collective-permute-start.3 = (bf16[2,80,128]{2,1,0:T(8,128)(2,1)S(1)}, bf16[2,80,128]{2,1,0:T(8,128)(2,1)S(1)}, u32[]{:S(2)}, u32[]{:S(2)}) collective-permute-start(bf16[2,80,128]{2,1,0:T(8,128)(2,1)S(1)} %fusion.9), channel_id=1, source_target_pairs={{16,0},{32,16},{48,32},{64,48},{80,64},{96,80},{112,96},{17,1},{33... | collective-permute-start | bytes 122888 | tf_op jit(solution)/shard_map/ppermute | solution.py:387
  37.4 57.0 %copy-start.1 = (bf16[3,2048,128]{2,1,0:T(8,128)(2,1)S(1)}, bf16[3,2048,128]{2,1,0:T(8,128)(2,1)}, u32[]{:S(2)}) copy-start(bf16[3,2048,128]{2,1,0:T(8,128)(2,1)} %weight.4) | copy-start | bytes 4718596
  37.4 28.4 %collective-permute-start.4 = (bf16[4,2048,128]{2,1,0:T(8,128)(2,1)S(1)}, bf16[4,2048,128]{2,1,0:T(8,128)(2,1)S(1)}, u32[]{:S(2)}, u32[]{:S(2)}) collective-permute-start(bf16[4,2048,128]{2,1,0:T(8,128)(2,1)S(1)} %all-to-all-done.own), channel_id=1, source_target_pairs={{0,1},{1,0},{2,3},{3,2},{4,5},{5,4},{6,7},{7,6},{8,9},{9,8},{10,11... | collective-permute-start | bytes 6291464 | tf_op jit(solution)/shard_map/ppermute | solution.py:406
  65.8 39.4 %copy-start.2 = (bf16[128,2048]{1,0:T(8,128)(2,1)S(1)}, bf16[128,2048]{1,0:T(8,128)(2,1)}, u32[]{:S(2)}) copy-start(bf16[128,2048]{1,0:T(8,128)(2,1)} %weight.5) | copy-start | bytes 1572868
  93.0 1.3 collective-permute-start.5
  105.8 46.4 %copy-start = (bf16[2,128,4,16,128]{4,3,2,1,0:T(8,128)(2,1)S(1)}, bf16[2,128,4,16,128]{4,3,2,1,0:T(8,128)(2,1)}, u32[]{:S(2)}) copy-start(bf16[2,128,4,16,128]{4,3,2,1,0:T(8,128)(2,1)} %get-tuple-element.19.features) | copy-start | bytes 12582916

commit v3 on v2

--- a/solution.py
+++ b/solution.py
@@ -13,8 +13,8 @@
 EPS = 1e-06
 ROW = ("z", "xl")
 COL = ("xh", "y", "core")
+ACROSS = ("core", "y", "xh")
 ROWY = ("xl", "y", "z")
-PLANE = ("xh", "y")
 SAME = ("y", "xh", "xl", "z")
 EVERY = ROW + COL
 SWAP = [(0, 1), (1, 0)]
@@ -245,10 +245,14 @@
     )(*near(terms, *base))
 
 
-def qkv_kernel(own, other, weight, queries, pairs):
+def qkv_kernel(embedded, weight, queries, pairs):
     normed = []
-    for group in (own, other):
-        blocks = [group[pair, feature].astype(F32) for pair in range(8) for feature in range(2)]
+    for core in range(2):
+        blocks = [
+            embedded[core * 8 + pair % 4 * 2 + pair // 4, feature].astype(F32)
+            for pair in range(8)
+            for feature in range(2)
+        ]
         square = sum(block * block for block in blocks)
         square = jnp.sum(square, axis=-1, keepdims=True)
         scale = lax.rsqrt(square * (1.0 / 2048.0) + EPS)
@@ -261,13 +265,13 @@
             pairs[r, part] = result
 
 
-def project_qkv(own, other, weight):
+def project_qkv(embedded, weight):
     return pl.pallas_call(
         qkv_kernel,
         out_shape=[pltpu.VMEM((64, C), BF), pltpu.VMEM((8, 2, 64, C), BF)],
         compiler_params=params(),
         name="qkv",
-    )(*near(own, other, weight))
+    )(*near(embedded, weight))
 
 
 def attend_kernel(queries, pairs, weight, out):
@@ -280,10 +284,9 @@
     weights = (scores / jnp.sum(scores, axis=-1, keepdims=True)).astype(BF)
     attended = jnp.dot(weights, values, preferred_element_type=F32).astype(BF)
     projected = jnp.dot(attended, weight[...], preferred_element_type=F32).astype(BF)
-    core = lax.axis_index("core")
     for pair in range(8):
         for which in range(2):
-            target = pair * 2 + (core if which == 0 else 1 - core)
+            target = which * 8 + pair % 4 * 2 + pair // 4
             for feature in range(2):
                 at = (pair * 2 + feature) * C
                 out[target, feature] = projected[which * 32 : which * 32 + 32, at : at + C]
@@ -405,11 +408,10 @@
     own, patches = lax.optimization_barrier((own, patches))
     other = lax.ppermute(own, "core", SWAP)
     partial = embed(exchange(patches, SAME), own, other)
-    copies, embedded = sum_and_copy(8, exchange(partial, ROWY))
-    group = exchange(copies, PLANE)
-    queries, pairs = project_qkv(group, lax.ppermute(group, "core", SWAP), qkv_weight)
+    copies, embedded = sum_and_copy(16, exchange(partial, ROWY))
+    queries, pairs = project_qkv(exchange(copies, ACROSS), qkv_weight)
     projected = attend(queries, exchange(pairs, ROW), out_weight)
-    copies, _ = sum_and_copy(32, exchange(projected, COL), embedded)
+    copies, _ = sum_and_copy(32, exchange(projected, ACROSS), embedded)
     patch_values = unembed(exchange(copies, ROWY), own, other)
     return finish(features, exchange(patch_values, SAME))
 

time: 155 us -> 155 us (level)
  transfers between devices with their start and end apart: 7 -> 6, of which waited for: 5 -> 4; matrix products, arithmetic and copies ran while one was open for 1% -> 1% of each run, Pallas kernels for 10% -> 10%
where the time goes in v3:
time: 155 us; the launch traced here: 154 us
  blocking collectives  106 us (68%)
  Pallas kernels  21 us (14%)
  starting transfers between devices  17.9 us (12%)
  waiting for transfers between devices  6.63 us (4%)
  local copies, waits for them, and re-layouts  2.25 us (1%)
    all_to_all x7, blocking collectives, exchange(): return lax.all_to_all(array, axes, 0, 0, tiled=True)  106 us
    pallas_call x1, Pallas kernels, convolve(): pl.pallas_call(conv_kernel, grid=(2, steps), in_specs=[pl.BlockSpec((1, C...  12.4 us
    all_to_all x1, starting transfers between devices, exchange(): return lax.all_to_all(array, axes, 0, 0, tiled=True)  6.31 us
    ppermute x2, waiting for transfers between devices, from_neighbours(): lax.ppermute(high, axes, backward)  5.5 us
    ppermute x2, starting transfers between devices, from_neighbours(): lax.ppermute(low, axes, forward)  4.69 us
    ppermute x1, starting transfers between devices, on_device(): other = lax.ppermute(own, 'core', SWAP)  4.27 us
  transfers between devices with their start and end apart: 6, of which 4 were waited for; matrix products, arithmetic and copies ran while one was open for 1% of the time, Pallas kernels for 10%

profile of v3, /device:TPU:0, one launch (start us, length us, event | category | flops | bytes accessed | tf_op | source)
XLA Modules:
  0.0 154.0 jit_solution(6626981786027142950)
XLA Ops:
  0.0 1.4 fusion.10
  1.4 1.3 collective-permute-start
  2.8 1.3 collective-permute-start.1
  4.1 0.0 copy-start.3
  4.1 2.5 %pack.1 = bf16[4,2048,128]{2,1,0:T(8,128)(2,1)} custom-call(bf16[4,1024,128]{2,1,0:T(8,128)(2,1)} %bitcast.16, bf16[4,1024,128]{2,1,0:T(8,128)(2,1)} %bitcast.17), custom_call_target="tpu_custom_call" | custom-call | tf_op jit(solution)/shard_map/pack/pallas_call | solution.py:67
  6.6 0.0 collective-permute-done.left
  6.6 1.2 collective-permute-done.1.right
  7.8 6.3 %all-to-all-start = ((bf16[4,2048,128]{2,1,0:T(8,128)(2,1)}), bf16[4,2048,128]{2,1,0:T(8,128)(2,1)S(1)}, u32[]{:S(2)}, u32[]{:S(2)}) async-start(bf16[4,2048,128]{2,1,0:T(8,128)(2,1)} %pack.1), calls=%async_computation | async-start | bytes 4194304 | tf_op jit(solution)/shard_map/all_to_all | solution.py:384
  14.1 0.8 slice_bitcast_fusion
  14.9 3.4 %collective-permute-start.2 = (bf16[2,80,128]{2,1,0:T(8,128)(2,1)S(1)}, bf16[2,80,128]{2,1,0:T(8,128)(2,1)S(1)}, u32[]{:S(2)}, u32[]{:S(2)}) collective-permute-start(bf16[2,80,128]{2,1,0:T(8,128)(2,1)S(1)} %fusion.7), channel_id=1, source_target_pairs={{0,16},{16,32},{32,48},{48,64},{64,80},{80,96},{96,112},{1,17},{17... | collective-permute-start | bytes 122888 | tf_op jit(solution)/shard_map/ppermute | solution.py:390
  18.4 1.3 collective-permute-start.3
  19.7 0.3 collective-permute-done.2.top
  20.0 4.3 %collective-permute-done.3.bottom = bf16[2,80,128]{2,1,0:T(8,128)(2,1)S(1)} collective-permute-done((bf16[2,80,128]{2,1,0:T(8,128)(2,1)S(1)}, bf16[2,80,128]{2,1,0:T(8,128)(2,1)S(1)}, u32[]{:S(2)}, u32[]{:S(2)}) %collective-permute-start.3) | collective-permute-done | bytes 40992 | tf_op jit(solution)/shard_map/ppermute | solution.py:390
  24.2 0.0 copy-done.3
  24.2 12.4 %conv_block.1 = (bf16[2,128,4,16,128]{4,3,2,1,0:T(8,128)(2,1)}, bf16[64,32,128]{2,1,0:T(8,128)(2,1)S(1)}) custom-call(bf16[2,128,64,128]{3,2,1,0:T(8,128)(2,1)} %below.1, bf16[2,128,64,128]{3,2,1,0:T(8,128)(2,1)} %below.1, bf16[2,128,64,128]{3,2,1,0:T(8,128)(2,1)} %below.1, bf16[2,80,128]{2,1,0:T(8,128)(2,1)S(1)} %collective-permute-done.2.top, ...), custom_call_target="tpu_custom_call" | custom-call | flops 4831838208 | bytes 9437184 | tf_op jit(solution)/shard_map/conv_block/pallas_call | solution.py:167
  36.6 0.8 all-to-all-done.own
  37.4 0.0 copy-start.1
  37.4 4.3 %collective-permute-start.4 = (bf16[4,2048,128]{2,1,0:T(8,128)(2,1)S(1)}, bf16[4,2048,128]{2,1,0:T(8,128)(2,1)S(1)}, u32[]{:S(2)}, u32[]{:S(2)}) collective-permute-start(bf16[4,2048,128]{2,1,0:T(8,128)(2,1)S(1)} %all-to-all-done.own), channel_id=1, source_target_pairs={{0,1},{1,0},{2,3},{3,2},{4,5},{5,4},{6,7},{7,6},{8,9},{9,8},{10,11... | collective-permute-start | bytes 6291464 | tf_op jit(solution)/shard_map/ppermute | solution.py:409
  41.7 24.1 %all_to_all.40.received = bf16[64,32,128]{2,1,0:T(8,128)(2,1)S(1)} all-to-all(bf16[64,32,128]{2,1,0:T(8,128)(2,1)S(1)} %get-tuple-element.22), channel_id=1, replica_groups=mesh['z'=4,'xl'=2,'xh'=2,'y'=4,'core'=2] {'y','xh','xl','z'}, dimensions={0} | all-to-all | bytes 1048576 | tf_op jit(solution)/shard_map/all_to_all | solution.py:384
  65.8 0.0 copy-start.2
  65.8 0.0 collective-permute-done.4.other
  65.8 0.8 embed.1
  66.6 13.7 %all_to_all.41.terms = bf16[32,2,32,128]{3,2,1,0:T(8,128)(2,1)S(1)} all-to-all(bf16[32,2,32,128]{3,2,1,0:T(8,128)(2,1)S(1)} %embed.1), channel_id=1, replica_groups=mesh['z'=4,'xl'=2,'xh'=2,'y'=4,'core'=2] {'xl','y','z'}, dimensions={0} | all-to-all | bytes 1048576 | tf_op jit(solution)/shard_map/all_to_all | solution.py:384
  80.3 0.1 sum_and_copy.2
  80.4 14.1 %all_to_all.42.embedded = bf16[16,2,32,128]{3,2,1,0:T(8,128)(2,1)S(1)} all-to-all(bf16[16,2,32,128]{3,2,1,0:T(8,128)(2,1)S(1)} %get-tuple-element.24), channel_id=1, replica_groups=mesh['z'=4,'xl'=2,'xh'=2,'y'=4,'core'=2] {'core','y','xh'}, dimensions={0} | all-to-all | bytes 524288 | tf_op jit(solution)/shard_map/all_to_all | solution.py:384
  94.6 0.0 copy-done.1
  94.6 0.5 qkv.1
  95.0 9.7 %all_to_all.43.pairs = bf16[8,2,64,128]{3,2,1,0:T(8,128)(2,1)S(1)} all-to-all(bf16[8,2,64,128]{3,2,1,0:T(8,128)(2,1)S(1)} %get-tuple-element.26), channel_id=1, replica_groups=mesh['z'=4,'xl'=2,'xh'=2,'y'=4,'core'=2] {'z','xl'}, dimensions={0} | all-to-all | bytes 524288 | tf_op jit(solution)/shard_map/all_to_all | solution.py:384
  104.7 0.0 copy-done.2
  104.7 0.7 attend.1
  105.4 0.0 copy-start
  105.4 12.6 %all_to_all.44.terms = bf16[16,2,32,128]{3,2,1,0:T(8,128)(2,1)S(1)} all-to-all(bf16[16,2,32,128]{3,2,1,0:T(8,128)(2,1)S(1)} %attend.1), channel_id=1, replica_groups=mesh['z'=4,'xl'=2,'xh'=2,'y'=4,'core'=2] {'core','y','xh'}, dimensions={0} | all-to-all | bytes 524288 | tf_op jit(solution)/shard_map/all_to_all | solution.py:384
  118.0 0.7 sum_and_copy.3
  118.7 14.8 %all_to_all.45.mixed = bf16[32,2,32,128]{3,2,1,0:T(8,128)(2,1)S(1)} all-to-all(bf16[32,2,32,128]{3,2,1,0:T(8,128)(2,1)S(1)} %get-tuple-element.28), channel_id=1, replica_groups=mesh['z'=4,'xl'=2,'xh'=2,'y'=4,'core'=2] {'xl','y','z'}, dimensions={0} | all-to-all | bytes 1048576 | tf_op jit(solution)/shard_map/all_to_all | solution.py:384
  133.5 0.8 unembed.1
  134.3 17.1 %all_to_all.46.received = bf16[64,32,128]{2,1,0:T(8,128)(2,1)S(1)} all-to-all(bf16[64,32,128]{2,1,0:T(8,128)(2,1)S(1)} %unembed.1), channel_id=1, replica_groups=mesh['z'=4,'xl'=2,'xh'=2,'y'=4,'core'=2] {'y','xh','xl','z'}, dimensions={0} | all-to-all | bytes 1048576 | tf_op jit(solution)/shard_map/all_to_all | solution.py:384
  151.4 0.0 copy-done
  151.4 2.6 %finish.1 = bf16[2,128,64,128]{3,2,1,0:T(8,128)(2,1)} custom-call(bf16[2,128,4,16,128]{4,3,2,1,0:T(8,128)(2,1)S(1)} %copy-done, bf16[64,32,128]{2,1,0:T(8,128)(2,1)S(1)} %all_to_all.46.received), custom_call_target="tpu_custom_call" | custom-call | tf_op jit(solution)/shard_map/finish/pallas_call | solution.py:368
  (5 shorter events, 0.1 us)
Async XLA Ops:
  1.4 5.1 %collective-permute-start = (bf16[2,128,128]{2,1,0:T(8,128)(2,1)S(1)}, bf16[2,128,128]{2,1,0:T(8,128)(2,1)S(1)}, u32[]{:S(2)}, u32[]{:S(2)}) collective-permute-start(bf16[2,128,128]{2,1,0:T(8,128)(2,1)S(1)} %bitcast.18), channel_id=1, source_target_pairs={{0,1},{1,2},{2,3},{3,4},{4,5},{5,6},{6,7},{7,8},{8,9},{9,10},{10,1... | collective-permute-start | bytes 196616 | tf_op jit(solution)/shard_map/ppermute | solution.py:390
  2.8 5.0 %collective-permute-start.1 = (bf16[2,128,128]{2,1,0:T(8,128)(2,1)S(1)}, bf16[2,128,128]{2,1,0:T(8,128)(2,1)S(1)}, u32[]{:S(2)}, u32[]{:S(2)}) collective-permute-start(bf16[2,128,128]{2,1,0:T(8,128)(2,1)S(1)} %bitcast.19), channel_id=1, source_target_pairs={{1,0},{2,1},{3,2},{4,3},{5,4},{6,5},{7,6},{8,7},{9,8},{10,9},{11,1... | collective-permute-start | bytes 196616 | tf_op jit(solution)/shard_map/ppermute | solution.py:390
  4.1 20.2 %copy-start.3 = (bf16[3,3,128,128]{3,2,1,0:T(8,128)(2,1)S(1)}, bf16[3,3,128,128]{3,2,1,0:T(8,128)(2,1)}, u32[]{:S(2)}) copy-start(bf16[3,3,128,128]{3,2,1,0:T(8,128)(2,1)} %weight.3) | copy-start | bytes 884740
  7.8 29.6 %all-to-all-start = ((bf16[4,2048,128]{2,1,0:T(8,128)(2,1)}), bf16[4,2048,128]{2,1,0:T(8,128)(2,1)S(1)}, u32[]{:S(2)}, u32[]{:S(2)}) async-start(bf16[4,2048,128]{2,1,0:T(8,128)(2,1)} %pack.1), calls=%async_computation | async-start | bytes 4194304 | tf_op jit(solution)/shard_map/all_to_all | solution.py:384
  14.9 5.1 %collective-permute-start.2 = (bf16[2,80,128]{2,1,0:T(8,128)(2,1)S(1)}, bf16[2,80,128]{2,1,0:T(8,128)(2,1)S(1)}, u32[]{:S(2)}, u32[]{:S(2)}) collective-permute-start(bf16[2,80,128]{2,1,0:T(8,128)(2,1)S(1)} %fusion.7), channel_id=1, source_target_pairs={{0,16},{16,32},{32,48},{48,64},{64,80},{80,96},{96,112},{1,17},{17... | collective-permute-start | bytes 122888 | tf_op jit(solution)/shard_map/ppermute | solution.py:390
  18.4 5.9 %collective-permute-start.3 = (bf16[2,80,128]{2,1,0:T(8,128)(2,1)S(1)}, bf16[2,80,128]{2,1,0:T(8,128)(2,1)S(1)}, u32[]{:S(2)}, u32[]{:S(2)}) collective-permute-start(bf16[2,80,128]{2,1,0:T(8,128)(2,1)S(1)} %fusion.9), channel_id=1, source_target_pairs={{16,0},{32,16},{48,32},{64,48},{80,64},{96,80},{112,96},{17,1},{33... | collective-permute-start | bytes 122888 | tf_op jit(solution)/shard_map/ppermute | solution.py:390
  37.4 57.2 %copy-start.1 = (bf16[3,2048,128]{2,1,0:T(8,128)(2,1)S(1)}, bf16[3,2048,128]{2,1,0:T(8,128)(2,1)}, u32[]{:S(2)}) copy-start(bf16[3,2048,128]{2,1,0:T(8,128)(2,1)} %weight.4) | copy-start | bytes 4718596
  37.4 28.4 %collective-permute-start.4 = (bf16[4,2048,128]{2,1,0:T(8,128)(2,1)S(1)}, bf16[4,2048,128]{2,1,0:T(8,128)(2,1)S(1)}, u32[]{:S(2)}, u32[]{:S(2)}) collective-permute-start(bf16[4,2048,128]{2,1,0:T(8,128)(2,1)S(1)} %all-to-all-done.own), channel_id=1, source_target_pairs={{0,1},{1,0},{2,3},{3,2},{4,5},{5,4},{6,7},{7,6},{8,9},{9,8},{10,11... | collective-permute-start | bytes 6291464 | tf_op jit(solution)/shard_map/ppermute | solution.py:409
  65.8 39.0 %copy-start.2 = (bf16[128,2048]{1,0:T(8,128)(2,1)S(1)}, bf16[128,2048]{1,0:T(8,128)(2,1)}, u32[]{:S(2)}) copy-start(bf16[128,2048]{1,0:T(8,128)(2,1)} %weight.5) | copy-start | bytes 1572868
  105.4 46.0 %copy-start = (bf16[2,128,4,16,128]{4,3,2,1,0:T(8,128)(2,1)S(1)}, bf16[2,128,4,16,128]{4,3,2,1,0:T(8,128)(2,1)}, u32[]{:S(2)}) copy-start(bf16[2,128,4,16,128]{4,3,2,1,0:T(8,128)(2,1)} %get-tuple-element.19.features) | copy-start | bytes 12582916

commit v4 on v3

--- a/solution.py
+++ b/solution.py
@@ -20,7 +20,7 @@
 SWAP = [(0, 1), (1, 0)]
 CHUNK = 64
 SPREAD = 128
-SUB = 16
+SUB = 8
 LEFT = 8
 
 
@@ -215,7 +215,7 @@
         embed_kernel,
         out_shape=pltpu.VMEM((32, 2, 32, C), BF),
         scratch_shapes=[
-            pltpu.VMEM((2048, C), F32),
+            pltpu.VMEM((2048 + 8, C), F32),
             pltpu.VMEM((256, 1024), BF),
         ],
         compiler_params=params(),
@@ -334,7 +334,7 @@
         out_shape=pltpu.VMEM((64, 32, C), BF),
         scratch_shapes=[
             pltpu.VMEM((256, 1024), BF),
-            pltpu.VMEM((2048, C), F32),
+            pltpu.VMEM((2048 + 8, C), F32),
         ],
         compiler_params=params(),
         name="unembed",
@@ -361,7 +361,7 @@
             for m in range(4):
                 value = features[frame, step * SPREAD + q * 4 + row, m].astype(F32) + small
                 spread[q * 4 + row, pl.ds(m, 16, stride=4), :] = value
-    out[0] = spread[...].astype(BF)
+    out[0] = spread[:, pl.ds(0, 64), :].astype(BF)
 
 
 def finish(features, received):
@@ -373,7 +373,7 @@
         out_shape=jax.ShapeDtypeStruct((2, 128, 64, C), BF),
         scratch_shapes=[
             pltpu.VMEM((32, 32, C), F32),
-            pltpu.VMEM((SPREAD, 64, C), F32),
+            pltpu.VMEM((SPREAD, 64 + 8, C), F32),
         ],
         compiler_params=params(),
         name="finish",

time: 155 us -> 154 us (level)
  transfers between devices with their start and end apart: 6 -> 6, of which waited for: 4 -> 4; matrix products, arithmetic and copies ran while one was open for 1% -> 1% of each run, Pallas kernels for 10% -> 9%
where the time goes in v4:
time: 154 us
  blocking collectives  106 us (69%)
  Pallas kernels  20.7 us (13%)
  starting transfers between devices  17.9 us (12%)
  waiting for transfers between devices  6.95 us (5%)
  local copies, waits for them, and re-layouts  2.25 us (1%)
    all_to_all x7, blocking collectives, exchange(): return lax.all_to_all(array, axes, 0, 0, tiled=True)  106 us
    pallas_call x1, Pallas kernels, convolve(): pl.pallas_call(conv_kernel, grid=(2, steps), in_specs=[pl.BlockSpec((1, C...  12 us
    all_to_all x1, starting transfers between devices, exchange(): return lax.all_to_all(array, axes, 0, 0, tiled=True)  6.31 us
    ppermute x2, waiting for transfers between devices, from_neighbours(): lax.ppermute(high, axes, backward)  5.5 us
    ppermute x2, starting transfers between devices, from_neighbours(): lax.ppermute(low, axes, forward)  4.69 us
    ppermute x1, starting transfers between devices, on_device(): other = lax.ppermute(own, 'core', SWAP)  4.27 us
  transfers between devices with their start and end apart: 6, of which 4 were waited for; matrix products, arithmetic and copies ran while one was open for 1% of the time, Pallas kernels for 9%

profile of v4, /device:TPU:0, one launch (start us, length us, event | category | flops | bytes accessed | tf_op | source)
XLA Modules:
  0.0 153.7 jit_solution(8751083831298931594)
XLA Ops:
  0.0 1.4 fusion.10
  1.4 1.3 collective-permute-start
  2.8 1.3 collective-permute-start.1
  4.1 0.0 copy-start.3
  4.1 2.5 %pack.1 = bf16[4,2048,128]{2,1,0:T(8,128)(2,1)} custom-call(bf16[4,1024,128]{2,1,0:T(8,128)(2,1)} %bitcast.16, bf16[4,1024,128]{2,1,0:T(8,128)(2,1)} %bitcast.17), custom_call_target="tpu_custom_call" | custom-call | tf_op jit(solution)/shard_map/pack/pallas_call | solution.py:67
  6.6 0.0 collective-permute-done.left
  6.6 1.2 collective-permute-done.1.right
  7.8 6.3 %all-to-all-start = ((bf16[4,2048,128]{2,1,0:T(8,128)(2,1)}), bf16[4,2048,128]{2,1,0:T(8,128)(2,1)S(1)}, u32[]{:S(2)}, u32[]{:S(2)}) async-start(bf16[4,2048,128]{2,1,0:T(8,128)(2,1)} %pack.1), calls=%async_computation | async-start | bytes 4194304 | tf_op jit(solution)/shard_map/all_to_all | solution.py:384
  14.1 0.8 slice_bitcast_fusion
  14.9 3.4 %collective-permute-start.2 = (bf16[2,80,128]{2,1,0:T(8,128)(2,1)S(1)}, bf16[2,80,128]{2,1,0:T(8,128)(2,1)S(1)}, u32[]{:S(2)}, u32[]{:S(2)}) collective-permute-start(bf16[2,80,128]{2,1,0:T(8,128)(2,1)S(1)} %fusion.7), channel_id=1, source_target_pairs={{0,16},{16,32},{32,48},{48,64},{64,80},{80,96},{96,112},{1,17},{17... | collective-permute-start | bytes 122888 | tf_op jit(solution)/shard_map/ppermute | solution.py:390
  18.4 1.3 collective-permute-start.3
  19.7 0.3 collective-permute-done.2.top
  20.0 4.3 %collective-permute-done.3.bottom = bf16[2,80,128]{2,1,0:T(8,128)(2,1)S(1)} collective-permute-done((bf16[2,80,128]{2,1,0:T(8,128)(2,1)S(1)}, bf16[2,80,128]{2,1,0:T(8,128)(2,1)S(1)}, u32[]{:S(2)}, u32[]{:S(2)}) %collective-permute-start.3) | collective-permute-done | bytes 40992 | tf_op jit(solution)/shard_map/ppermute | solution.py:390
  24.2 0.0 copy-done.3
  24.2 12.0 %conv_block.1 = (bf16[2,128,4,16,128]{4,3,2,1,0:T(8,128)(2,1)}, bf16[64,32,128]{2,1,0:T(8,128)(2,1)S(1)}) custom-call(bf16[2,128,64,128]{3,2,1,0:T(8,128)(2,1)} %below.1, bf16[2,128,64,128]{3,2,1,0:T(8,128)(2,1)} %below.1, bf16[2,128,64,128]{3,2,1,0:T(8,128)(2,1)} %below.1, bf16[2,80,128]{2,1,0:T(8,128)(2,1)S(1)} %collective-permute-done.2.top, ...), custom_call_target="tpu_custom_call" | custom-call | flops 4831838208 | bytes 9437184 | tf_op jit(solution)/shard_map/conv_block/pallas_call | solution.py:167
  36.3 1.1 all-to-all-done.own
  37.4 0.0 copy-start.1
  37.4 4.3 %collective-permute-start.4 = (bf16[4,2048,128]{2,1,0:T(8,128)(2,1)S(1)}, bf16[4,2048,128]{2,1,0:T(8,128)(2,1)S(1)}, u32[]{:S(2)}, u32[]{:S(2)}) collective-permute-start(bf16[4,2048,128]{2,1,0:T(8,128)(2,1)S(1)} %all-to-all-done.own), channel_id=1, source_target_pairs={{0,1},{1,0},{2,3},{3,2},{4,5},{5,4},{6,7},{7,6},{8,9},{9,8},{10,11... | collective-permute-start | bytes 6291464 | tf_op jit(solution)/shard_map/ppermute | solution.py:409
  41.7 23.8 %all_to_all.40.received = bf16[64,32,128]{2,1,0:T(8,128)(2,1)S(1)} all-to-all(bf16[64,32,128]{2,1,0:T(8,128)(2,1)S(1)} %get-tuple-element.22), channel_id=1, replica_groups=mesh['z'=4,'xl'=2,'xh'=2,'y'=4,'core'=2] {'y','xh','xl','z'}, dimensions={0} | all-to-all | bytes 1048576 | tf_op jit(solution)/shard_map/all_to_all | solution.py:384
  65.5 0.0 copy-start.2
  65.5 0.0 collective-permute-done.4.other
  65.5 0.8 embed.1
  66.3 13.7 %all_to_all.41.terms = bf16[32,2,32,128]{3,2,1,0:T(8,128)(2,1)S(1)} all-to-all(bf16[32,2,32,128]{3,2,1,0:T(8,128)(2,1)S(1)} %embed.1), channel_id=1, replica_groups=mesh['z'=4,'xl'=2,'xh'=2,'y'=4,'core'=2] {'xl','y','z'}, dimensions={0} | all-to-all | bytes 1048576 | tf_op jit(solution)/shard_map/all_to_all | solution.py:384
  80.0 0.1 sum_and_copy.2
  80.1 14.1 %all_to_all.42.embedded = bf16[16,2,32,128]{3,2,1,0:T(8,128)(2,1)S(1)} all-to-all(bf16[16,2,32,128]{3,2,1,0:T(8,128)(2,1)S(1)} %get-tuple-element.24), channel_id=1, replica_groups=mesh['z'=4,'xl'=2,'xh'=2,'y'=4,'core'=2] {'core','y','xh'}, dimensions={0} | all-to-all | bytes 524288 | tf_op jit(solution)/shard_map/all_to_all | solution.py:384
  94.2 0.0 copy-done.1
  94.2 0.5 qkv.1
  94.7 9.7 %all_to_all.43.pairs = bf16[8,2,64,128]{3,2,1,0:T(8,128)(2,1)S(1)} all-to-all(bf16[8,2,64,128]{3,2,1,0:T(8,128)(2,1)S(1)} %get-tuple-element.26), channel_id=1, replica_groups=mesh['z'=4,'xl'=2,'xh'=2,'y'=4,'core'=2] {'z','xl'}, dimensions={0} | all-to-all | bytes 524288 | tf_op jit(solution)/shard_map/all_to_all | solution.py:384
  104.4 0.0 copy-done.2
  104.4 0.7 attend.1
  105.1 0.0 copy-start
  105.1 12.5 %all_to_all.44.terms = bf16[16,2,32,128]{3,2,1,0:T(8,128)(2,1)S(1)} all-to-all(bf16[16,2,32,128]{3,2,1,0:T(8,128)(2,1)S(1)} %attend.1), channel_id=1, replica_groups=mesh['z'=4,'xl'=2,'xh'=2,'y'=4,'core'=2] {'core','y','xh'}, dimensions={0} | all-to-all | bytes 524288 | tf_op jit(solution)/shard_map/all_to_all | solution.py:384
  117.7 0.7 sum_and_copy.3
  118.3 14.8 %all_to_all.45.mixed = bf16[32,2,32,128]{3,2,1,0:T(8,128)(2,1)S(1)} all-to-all(bf16[32,2,32,128]{3,2,1,0:T(8,128)(2,1)S(1)} %get-tuple-element.28), channel_id=1, replica_groups=mesh['z'=4,'xl'=2,'xh'=2,'y'=4,'core'=2] {'xl','y','z'}, dimensions={0} | all-to-all | bytes 1048576 | tf_op jit(solution)/shard_map/all_to_all | solution.py:384
  133.2 0.8 unembed.1
  134.0 17.1 %all_to_all.46.received = bf16[64,32,128]{2,1,0:T(8,128)(2,1)S(1)} all-to-all(bf16[64,32,128]{2,1,0:T(8,128)(2,1)S(1)} %unembed.1), channel_id=1, replica_groups=mesh['z'=4,'xl'=2,'xh'=2,'y'=4,'core'=2] {'y','xh','xl','z'}, dimensions={0} | all-to-all | bytes 1048576 | tf_op jit(solution)/shard_map/all_to_all | solution.py:384
  151.1 0.0 copy-done
  151.1 2.6 %finish.1 = bf16[2,128,64,128]{3,2,1,0:T(8,128)(2,1)} custom-call(bf16[2,128,4,16,128]{4,3,2,1,0:T(8,128)(2,1)S(1)} %copy-done, bf16[64,32,128]{2,1,0:T(8,128)(2,1)S(1)} %all_to_all.46.received), custom_call_target="tpu_custom_call" | custom-call | tf_op jit(solution)/shard_map/finish/pallas_call | solution.py:368
  (5 shorter events, 0.1 us)
Async XLA Ops:
  1.4 5.1 %collective-permute-start = (bf16[2,128,128]{2,1,0:T(8,128)(2,1)S(1)}, bf16[2,128,128]{2,1,0:T(8,128)(2,1)S(1)}, u32[]{:S(2)}, u32[]{:S(2)}) collective-permute-start(bf16[2,128,128]{2,1,0:T(8,128)(2,1)S(1)} %bitcast.18), channel_id=1, source_target_pairs={{0,1},{1,2},{2,3},{3,4},{4,5},{5,6},{6,7},{7,8},{8,9},{9,10},{10,1... | collective-permute-start | bytes 196616 | tf_op jit(solution)/shard_map/ppermute | solution.py:390
  2.8 5.0 %collective-permute-start.1 = (bf16[2,128,128]{2,1,0:T(8,128)(2,1)S(1)}, bf16[2,128,128]{2,1,0:T(8,128)(2,1)S(1)}, u32[]{:S(2)}, u32[]{:S(2)}) collective-permute-start(bf16[2,128,128]{2,1,0:T(8,128)(2,1)S(1)} %bitcast.19), channel_id=1, source_target_pairs={{1,0},{2,1},{3,2},{4,3},{5,4},{6,5},{7,6},{8,7},{9,8},{10,9},{11,1... | collective-permute-start | bytes 196616 | tf_op jit(solution)/shard_map/ppermute | solution.py:390
  4.1 20.2 %copy-start.3 = (bf16[3,3,128,128]{3,2,1,0:T(8,128)(2,1)S(1)}, bf16[3,3,128,128]{3,2,1,0:T(8,128)(2,1)}, u32[]{:S(2)}) copy-start(bf16[3,3,128,128]{3,2,1,0:T(8,128)(2,1)} %weight.3) | copy-start | bytes 884740
  7.8 29.6 %all-to-all-start = ((bf16[4,2048,128]{2,1,0:T(8,128)(2,1)}), bf16[4,2048,128]{2,1,0:T(8,128)(2,1)S(1)}, u32[]{:S(2)}, u32[]{:S(2)}) async-start(bf16[4,2048,128]{2,1,0:T(8,128)(2,1)} %pack.1), calls=%async_computation | async-start | bytes 4194304 | tf_op jit(solution)/shard_map/all_to_all | solution.py:384
  14.9 5.1 %collective-permute-start.2 = (bf16[2,80,128]{2,1,0:T(8,128)(2,1)S(1)}, bf16[2,80,128]{2,1,0:T(8,128)(2,1)S(1)}, u32[]{:S(2)}, u32[]{:S(2)}) collective-permute-start(bf16[2,80,128]{2,1,0:T(8,128)(2,1)S(1)} %fusion.7), channel_id=1, source_target_pairs={{0,16},{16,32},{32,48},{48,64},{64,80},{80,96},{96,112},{1,17},{17... | collective-permute-start | bytes 122888 | tf_op jit(solution)/shard_map/ppermute | solution.py:390
  18.4 5.9 %collective-permute-start.3 = (bf16[2,80,128]{2,1,0:T(8,128)(2,1)S(1)}, bf16[2,80,128]{2,1,0:T(8,128)(2,1)S(1)}, u32[]{:S(2)}, u32[]{:S(2)}) collective-permute-start(bf16[2,80,128]{2,1,0:T(8,128)(2,1)S(1)} %fusion.9), channel_id=1, source_target_pairs={{16,0},{32,16},{48,32},{64,48},{80,64},{96,80},{112,96},{17,1},{33... | collective-permute-start | bytes 122888 | tf_op jit(solution)/shard_map/ppermute | solution.py:390
  37.4 56.8 %copy-start.1 = (bf16[3,2048,128]{2,1,0:T(8,128)(2,1)S(1)}, bf16[3,2048,128]{2,1,0:T(8,128)(2,1)}, u32[]{:S(2)}) copy-start(bf16[3,2048,128]{2,1,0:T(8,128)(2,1)} %weight.4) | copy-start | bytes 4718596
  37.4 28.1 %collective-permute-start.4 = (bf16[4,2048,128]{2,1,0:T(8,128)(2,1)S(1)}, bf16[4,2048,128]{2,1,0:T(8,128)(2,1)S(1)}, u32[]{:S(2)}, u32[]{:S(2)}) collective-permute-start(bf16[4,2048,128]{2,1,0:T(8,128)(2,1)S(1)} %all-to-all-done.own), channel_id=1, source_target_pairs={{0,1},{1,0},{2,3},{3,2},{4,5},{5,4},{6,7},{7,6},{8,9},{9,8},{10,11... | collective-permute-start | bytes 6291464 | tf_op jit(solution)/shard_map/ppermute | solution.py:409
  65.5 39.0 %copy-start.2 = (bf16[128,2048]{1,0:T(8,128)(2,1)S(1)}, bf16[128,2048]{1,0:T(8,128)(2,1)}, u32[]{:S(2)}) copy-start(bf16[128,2048]{1,0:T(8,128)(2,1)} %weight.5) | copy-start | bytes 1572868
  105.1 46.0 %copy-start = (bf16[2,128,4,16,128]{4,3,2,1,0:T(8,128)(2,1)S(1)}, bf16[2,128,4,16,128]{4,3,2,1,0:T(8,128)(2,1)}, u32[]{:S(2)}) copy-start(bf16[2,128,4,16,128]{4,3,2,1,0:T(8,128)(2,1)} %get-tuple-element.19.features) | copy-start | bytes 12582916

commit v5 on v4

--- a/solution.py
+++ b/solution.py
@@ -14,7 +14,9 @@
 ROW = ("z", "xl")
 COL = ("xh", "y", "core")
 ACROSS = ("core", "y", "xh")
+GATHER = ("xl", "z", "y")
 ROWY = ("xl", "y", "z")
+PATCHES = ("xh", "y", "z", "xl")
 SAME = ("y", "xh", "xl", "z")
 EVERY = ROW + COL
 SWAP = [(0, 1), (1, 0)]
@@ -34,6 +36,14 @@
 
 def in_same(r, xh, y):
     return ((y * 2 + xh) * 2 + r % 2) * 4 + r // 2
+
+
+def in_patches(r, xh, y):
+    return (xh * 4 + y) * 8 + r
+
+
+def in_gather(r, y):
+    return (r % 2 * 4 + r // 2) * 4 + y
 
 
 def near(*arrays):
@@ -158,7 +168,7 @@
             for y in range(4):
                 block = pooled[r * 4 + y].astype(BF)
                 for xh in range(2):
-                    send[in_same(r, xh, y)] = block
+                    send[in_patches(r, xh, y)] = block
 
 
 def convolve(frames, top, bottom, left, right, weight):
@@ -198,7 +208,7 @@
         for xh in range(2):
             for y in range(4):
                 at = pl.ds(((r * 2 + xh) * 4 + y) * 32, 32)
-                rows[at, :] = received[in_same(r, xh, y)].astype(F32)
+                rows[at, :] = received[in_patches(r, xh, y)].astype(F32)
     for j in range(8):
         values[:, pl.ds(j * C, C)] = rows[pl.ds(j, 256, stride=8), :].astype(BF)
     for which, weight in enumerate((own, other)):
@@ -308,7 +318,7 @@
         for y in range(4):
             for r in range(8):
                 at = pl.ds((which * 4 + y) * C, C)
-                values[pl.ds(r * 32, 32), at] = mixed[in_rowy(r, y), feature]
+                values[pl.ds(r * 32, 32), at] = mixed[in_gather(r, y), feature]
     for pair in range(4):
         at = pl.ds(1024 + pair * 2 * C, 2 * C)
         wide = [weight[y, at] for weight in (own, other) for y in range(4)]
@@ -407,12 +417,12 @@
     features, patches = convolve(frames, top, bottom, left, right, conv_weight)
     own, patches = lax.optimization_barrier((own, patches))
     other = lax.ppermute(own, "core", SWAP)
-    partial = embed(exchange(patches, SAME), own, other)
+    partial = embed(exchange(patches, PATCHES), own, other)
     copies, embedded = sum_and_copy(16, exchange(partial, ROWY))
     queries, pairs = project_qkv(exchange(copies, ACROSS), qkv_weight)
     projected = attend(queries, exchange(pairs, ROW), out_weight)
     copies, _ = sum_and_copy(32, exchange(projected, ACROSS), embedded)
-    patch_values = unembed(exchange(copies, ROWY), own, other)
+    patch_values = unembed(exchange(copies, GATHER), own, other)
     return finish(features, exchange(patch_values, SAME))
 
 

time: 154 us -> 154 us (level)
  no operation moved by 1% of the time
where the time goes in v5:
time: 154 us; the launch traced here: 153 us
  blocking collectives  105 us (68%)
  Pallas kernels  20.7 us (13%)
  starting transfers between devices  17.9 us (12%)
  waiting for transfers between devices  6.95 us (5%)
  local copies, waits for them, and re-layouts  2.25 us (1%)
    all_to_all x7, blocking collectives, exchange(): return lax.all_to_all(array, axes, 0, 0, tiled=True)  105 us
    pallas_call x1, Pallas kernels, convolve(): pl.pallas_call(conv_kernel, grid=(2, steps), in_specs=[pl.BlockSpec((1, C...  12 us
    all_to_all x1, starting transfers between devices, exchange(): return lax.all_to_all(array, axes, 0, 0, tiled=True)  6.31 us
    ppermute x2, waiting for transfers between devices, from_neighbours(): lax.ppermute(high, axes, backward)  5.5 us
    ppermute x2, starting transfers between devices, from_neighbours(): lax.ppermute(low, axes, forward)  4.69 us
    ppermute x1, starting transfers between devices, on_device(): other = lax.ppermute(own, 'core', SWAP)  4.27 us
  transfers between devices with their start and end apart: 6, of which 4 were waited for; matrix products, arithmetic and copies ran while one was open for 1% of the time, Pallas kernels for 9%

profile of v5, /device:TPU:0, one launch (start us, length us, event | category | flops | bytes accessed | tf_op | source)
XLA Modules:
  0.0 153.1 jit_solution(12181550963177506865)
XLA Ops:
  0.0 1.4 fusion.10
  1.4 1.3 collective-permute-start
  2.8 1.3 collective-permute-start.1
  4.1 0.0 copy-start.3
  4.1 2.5 %pack.1 = bf16[4,2048,128]{2,1,0:T(8,128)(2,1)} custom-call(bf16[4,1024,128]{2,1,0:T(8,128)(2,1)} %bitcast.16, bf16[4,1024,128]{2,1,0:T(8,128)(2,1)} %bitcast.17), custom_call_target="tpu_custom_call" | custom-call | tf_op jit(solution)/shard_map/pack/pallas_call | solution.py:77
  6.6 0.0 collective-permute-done.left
  6.6 1.2 collective-permute-done.1.right
  7.8 6.3 %all-to-all-start = ((bf16[4,2048,128]{2,1,0:T(8,128)(2,1)}), bf16[4,2048,128]{2,1,0:T(8,128)(2,1)S(1)}, u32[]{:S(2)}, u32[]{:S(2)}) async-start(bf16[4,2048,128]{2,1,0:T(8,128)(2,1)} %pack.1), calls=%async_computation | async-start | bytes 4194304 | tf_op jit(solution)/shard_map/all_to_all | solution.py:394
  14.1 0.8 slice_bitcast_fusion
  14.9 3.4 %collective-permute-start.2 = (bf16[2,80,128]{2,1,0:T(8,128)(2,1)S(1)}, bf16[2,80,128]{2,1,0:T(8,128)(2,1)S(1)}, u32[]{:S(2)}, u32[]{:S(2)}) collective-permute-start(bf16[2,80,128]{2,1,0:T(8,128)(2,1)S(1)} %fusion.7), channel_id=1, source_target_pairs={{0,16},{16,32},{32,48},{48,64},{64,80},{80,96},{96,112},{1,17},{17... | collective-permute-start | bytes 122888 | tf_op jit(solution)/shard_map/ppermute | solution.py:400
  18.4 1.3 collective-permute-start.3
  19.7 0.3 collective-permute-done.2.top
  20.0 4.3 %collective-permute-done.3.bottom = bf16[2,80,128]{2,1,0:T(8,128)(2,1)S(1)} collective-permute-done((bf16[2,80,128]{2,1,0:T(8,128)(2,1)S(1)}, bf16[2,80,128]{2,1,0:T(8,128)(2,1)S(1)}, u32[]{:S(2)}, u32[]{:S(2)}) %collective-permute-start.3) | collective-permute-done | bytes 40992 | tf_op jit(solution)/shard_map/ppermute | solution.py:400
  24.2 0.0 copy-done.3
  24.2 12.0 %conv_block.1 = (bf16[2,128,4,16,128]{4,3,2,1,0:T(8,128)(2,1)}, bf16[64,32,128]{2,1,0:T(8,128)(2,1)S(1)}) custom-call(bf16[2,128,64,128]{3,2,1,0:T(8,128)(2,1)} %below.1, bf16[2,128,64,128]{3,2,1,0:T(8,128)(2,1)} %below.1, bf16[2,128,64,128]{3,2,1,0:T(8,128)(2,1)} %below.1, bf16[2,80,128]{2,1,0:T(8,128)(2,1)S(1)} %collective-permute-done.2.top, ...), custom_call_target="tpu_custom_call" | custom-call | flops 4831838208 | bytes 9437184 | tf_op jit(solution)/shard_map/conv_block/pallas_call | solution.py:177
  36.3 1.1 all-to-all-done.own
  37.4 0.0 copy-start.1
  37.4 4.3 %collective-permute-start.4 = (bf16[4,2048,128]{2,1,0:T(8,128)(2,1)S(1)}, bf16[4,2048,128]{2,1,0:T(8,128)(2,1)S(1)}, u32[]{:S(2)}, u32[]{:S(2)}) collective-permute-start(bf16[4,2048,128]{2,1,0:T(8,128)(2,1)S(1)} %all-to-all-done.own), channel_id=1, source_target_pairs={{0,1},{1,0},{2,3},{3,2},{4,5},{5,4},{6,7},{7,6},{8,9},{9,8},{10,11... | collective-permute-start | bytes 6291464 | tf_op jit(solution)/shard_map/ppermute | solution.py:419
  41.7 23.4 %all_to_all.40.received = bf16[64,32,128]{2,1,0:T(8,128)(2,1)S(1)} all-to-all(bf16[64,32,128]{2,1,0:T(8,128)(2,1)S(1)} %get-tuple-element.22), channel_id=1, replica_groups=mesh['z'=4,'xl'=2,'xh'=2,'y'=4,'core'=2] {'xh','y','z','xl'}, dimensions={0} | all-to-all | bytes 1048576 | tf_op jit(solution)/shard_map/all_to_all | solution.py:394
  65.0 0.0 copy-start.2
  65.0 0.0 collective-permute-done.4.other
  65.0 0.8 embed.1
  65.9 14.0 %all_to_all.41.terms = bf16[32,2,32,128]{3,2,1,0:T(8,128)(2,1)S(1)} all-to-all(bf16[32,2,32,128]{3,2,1,0:T(8,128)(2,1)S(1)} %embed.1), channel_id=1, replica_groups=mesh['z'=4,'xl'=2,'xh'=2,'y'=4,'core'=2] {'xl','y','z'}, dimensions={0} | all-to-all | bytes 1048576 | tf_op jit(solution)/shard_map/all_to_all | solution.py:394
  79.9 0.1 sum_and_copy.2
  80.0 13.6 %all_to_all.42.embedded = bf16[16,2,32,128]{3,2,1,0:T(8,128)(2,1)S(1)} all-to-all(bf16[16,2,32,128]{3,2,1,0:T(8,128)(2,1)S(1)} %get-tuple-element.24), channel_id=1, replica_groups=mesh['z'=4,'xl'=2,'xh'=2,'y'=4,'core'=2] {'core','y','xh'}, dimensions={0} | all-to-all | bytes 524288 | tf_op jit(solution)/shard_map/all_to_all | solution.py:394
  93.7 0.0 copy-done.1
  93.7 0.5 qkv.1
  94.1 9.7 %all_to_all.43.pairs = bf16[8,2,64,128]{3,2,1,0:T(8,128)(2,1)S(1)} all-to-all(bf16[8,2,64,128]{3,2,1,0:T(8,128)(2,1)S(1)} %get-tuple-element.26), channel_id=1, replica_groups=mesh['z'=4,'xl'=2,'xh'=2,'y'=4,'core'=2] {'z','xl'}, dimensions={0} | all-to-all | bytes 524288 | tf_op jit(solution)/shard_map/all_to_all | solution.py:394
  103.8 0.0 copy-done.2
  103.8 0.7 attend.1
  104.5 0.0 copy-start
  104.5 12.5 %all_to_all.44.terms = bf16[16,2,32,128]{3,2,1,0:T(8,128)(2,1)S(1)} all-to-all(bf16[16,2,32,128]{3,2,1,0:T(8,128)(2,1)S(1)} %attend.1), channel_id=1, replica_groups=mesh['z'=4,'xl'=2,'xh'=2,'y'=4,'core'=2] {'core','y','xh'}, dimensions={0} | all-to-all | bytes 524288 | tf_op jit(solution)/shard_map/all_to_all | solution.py:394
  117.1 0.7 sum_and_copy.3
  117.8 14.9 %all_to_all.45.mixed = bf16[32,2,32,128]{3,2,1,0:T(8,128)(2,1)S(1)} all-to-all(bf16[32,2,32,128]{3,2,1,0:T(8,128)(2,1)S(1)} %get-tuple-element.28), channel_id=1, replica_groups=mesh['z'=4,'xl'=2,'xh'=2,'y'=4,'core'=2] {'xl','z','y'}, dimensions={0} | all-to-all | bytes 1048576 | tf_op jit(solution)/shard_map/all_to_all | solution.py:394
  132.6 0.8 unembed.1
  133.5 17.1 %all_to_all.46.received = bf16[64,32,128]{2,1,0:T(8,128)(2,1)S(1)} all-to-all(bf16[64,32,128]{2,1,0:T(8,128)(2,1)S(1)} %unembed.1), channel_id=1, replica_groups=mesh['z'=4,'xl'=2,'xh'=2,'y'=4,'core'=2] {'y','xh','xl','z'}, dimensions={0} | all-to-all | bytes 1048576 | tf_op jit(solution)/shard_map/all_to_all | solution.py:394
  150.5 0.0 copy-done
  150.5 2.6 %finish.1 = bf16[2,128,64,128]{3,2,1,0:T(8,128)(2,1)} custom-call(bf16[2,128,4,16,128]{4,3,2,1,0:T(8,128)(2,1)S(1)} %copy-done, bf16[64,32,128]{2,1,0:T(8,128)(2,1)S(1)} %all_to_all.46.received), custom_call_target="tpu_custom_call" | custom-call | tf_op jit(solution)/shard_map/finish/pallas_call | solution.py:378
  (5 shorter events, 0.1 us)
Async XLA Ops:
  1.4 5.1 %collective-permute-start = (bf16[2,128,128]{2,1,0:T(8,128)(2,1)S(1)}, bf16[2,128,128]{2,1,0:T(8,128)(2,1)S(1)}, u32[]{:S(2)}, u32[]{:S(2)}) collective-permute-start(bf16[2,128,128]{2,1,0:T(8,128)(2,1)S(1)} %bitcast.18), channel_id=1, source_target_pairs={{0,1},{1,2},{2,3},{3,4},{4,5},{5,6},{6,7},{7,8},{8,9},{9,10},{10,1... | collective-permute-start | bytes 196616 | tf_op jit(solution)/shard_map/ppermute | solution.py:400
  2.8 5.0 %collective-permute-start.1 = (bf16[2,128,128]{2,1,0:T(8,128)(2,1)S(1)}, bf16[2,128,128]{2,1,0:T(8,128)(2,1)S(1)}, u32[]{:S(2)}, u32[]{:S(2)}) collective-permute-start(bf16[2,128,128]{2,1,0:T(8,128)(2,1)S(1)} %bitcast.19), channel_id=1, source_target_pairs={{1,0},{2,1},{3,2},{4,3},{5,4},{6,5},{7,6},{8,7},{9,8},{10,9},{11,1... | collective-permute-start | bytes 196616 | tf_op jit(solution)/shard_map/ppermute | solution.py:400
  4.1 20.2 %copy-start.3 = (bf16[3,3,128,128]{3,2,1,0:T(8,128)(2,1)S(1)}, bf16[3,3,128,128]{3,2,1,0:T(8,128)(2,1)}, u32[]{:S(2)}) copy-start(bf16[3,3,128,128]{3,2,1,0:T(8,128)(2,1)} %weight.3) | copy-start | bytes 884740
  7.8 29.6 %all-to-all-start = ((bf16[4,2048,128]{2,1,0:T(8,128)(2,1)}), bf16[4,2048,128]{2,1,0:T(8,128)(2,1)S(1)}, u32[]{:S(2)}, u32[]{:S(2)}) async-start(bf16[4,2048,128]{2,1,0:T(8,128)(2,1)} %pack.1), calls=%async_computation | async-start | bytes 4194304 | tf_op jit(solution)/shard_map/all_to_all | solution.py:394
  14.9 5.1 %collective-permute-start.2 = (bf16[2,80,128]{2,1,0:T(8,128)(2,1)S(1)}, bf16[2,80,128]{2,1,0:T(8,128)(2,1)S(1)}, u32[]{:S(2)}, u32[]{:S(2)}) collective-permute-start(bf16[2,80,128]{2,1,0:T(8,128)(2,1)S(1)} %fusion.7), channel_id=1, source_target_pairs={{0,16},{16,32},{32,48},{48,64},{64,80},{80,96},{96,112},{1,17},{17... | collective-permute-start | bytes 122888 | tf_op jit(solution)/shard_map/ppermute | solution.py:400
  18.4 5.9 %collective-permute-start.3 = (bf16[2,80,128]{2,1,0:T(8,128)(2,1)S(1)}, bf16[2,80,128]{2,1,0:T(8,128)(2,1)S(1)}, u32[]{:S(2)}, u32[]{:S(2)}) collective-permute-start(bf16[2,80,128]{2,1,0:T(8,128)(2,1)S(1)} %fusion.9), channel_id=1, source_target_pairs={{16,0},{32,16},{48,32},{64,48},{80,64},{96,80},{112,96},{17,1},{33... | collective-permute-start | bytes 122888 | tf_op jit(solution)/shard_map/ppermute | solution.py:400
  37.4 56.2 %copy-start.1 = (bf16[3,2048,128]{2,1,0:T(8,128)(2,1)S(1)}, bf16[3,2048,128]{2,1,0:T(8,128)(2,1)}, u32[]{:S(2)}) copy-start(bf16[3,2048,128]{2,1,0:T(8,128)(2,1)} %weight.4) | copy-start | bytes 4718596
  37.4 27.6 %collective-permute-start.4 = (bf16[4,2048,128]{2,1,0:T(8,128)(2,1)S(1)}, bf16[4,2048,128]{2,1,0:T(8,128)(2,1)S(1)}, u32[]{:S(2)}, u32[]{:S(2)}) collective-permute-start(bf16[4,2048,128]{2,1,0:T(8,128)(2,1)S(1)} %all-to-all-done.own), channel_id=1, source_target_pairs={{0,1},{1,0},{2,3},{3,2},{4,5},{5,4},{6,7},{7,6},{8,9},{9,8},{10,11... | collective-permute-start | bytes 6291464 | tf_op jit(solution)/shard_map/ppermute | solution.py:419
  65.0 38.8 %copy-start.2 = (bf16[128,2048]{1,0:T(8,128)(2,1)S(1)}, bf16[128,2048]{1,0:T(8,128)(2,1)}, u32[]{:S(2)}) copy-start(bf16[128,2048]{1,0:T(8,128)(2,1)} %weight.5) | copy-start | bytes 1572868
  104.5 46.0 %copy-start = (bf16[2,128,4,16,128]{4,3,2,1,0:T(8,128)(2,1)S(1)}, bf16[2,128,4,16,128]{4,3,2,1,0:T(8,128)(2,1)}, u32[]{:S(2)}) copy-start(bf16[2,128,4,16,128]{4,3,2,1,0:T(8,128)(2,1)} %get-tuple-element.19.features) | copy-start | bytes 12582916

commit v6 on v5

--- a/solution.py
+++ b/solution.py
@@ -233,26 +233,41 @@
     )(*near(received, own, other))
 
 
-def sum_kernel(copies, terms, *rest):
-    out, total_out = rest[-2:]
+def sum_kernel(copies, terms, out, total_out):
     total = terms[0].astype(F32)
     for i in range(1, terms.shape[0]):
         total = total + terms[i].astype(F32)
-    if len(rest) == 3:
-        total = rest[0][...].astype(F32) + total
     total = total.astype(BF)
     total_out[...] = total
     for i in range(copies):
         out[i] = total
 
 
-def sum_and_copy(copies, terms, *base):
+def sum_and_copy(copies, terms):
     return pl.pallas_call(
         functools.partial(sum_kernel, copies),
         out_shape=[pltpu.VMEM((copies, 2, 32, C), BF), pltpu.VMEM((2, 32, C), BF)],
         compiler_params=params(),
         name="sum_and_copy",
-    )(*near(terms, *base))
+    )(*near(terms))
+
+
+def mix_kernel(copies, terms, base, out):
+    total = base[...].astype(F32)
+    for i in range(terms.shape[0]):
+        total = total + terms[i].astype(F32)
+    total = total.astype(BF)
+    for i in range(copies):
+        out[i] = total
+
+
+def mix_and_copy(copies, terms, base):
+    return pl.pallas_call(
+        functools.partial(mix_kernel, copies),
+        out_shape=pltpu.VMEM((copies, 2, 32, C), BF),
+        compiler_params=params(),
+        name="mix_and_copy",
+    )(*near(terms, base))
 
 
 def qkv_kernel(embedded, weight, queries, pairs):
@@ -421,7 +436,7 @@
     copies, embedded = sum_and_copy(16, exchange(partial, ROWY))
     queries, pairs = project_qkv(exchange(copies, ACROSS), qkv_weight)
     projected = attend(queries, exchange(pairs, ROW), out_weight)
-    copies, _ = sum_and_copy(32, exchange(projected, ACROSS), embedded)
+    copies = mix_and_copy(32, exchange(projected, ACROSS), embedded)
     patch_values = unembed(exchange(copies, GATHER), own, other)
     return finish(features, exchange(patch_values, SAME))
 

time: 154 us -> 153 us (level)
  transfers between devices with their start and end apart: 6 -> 6, of which waited for: 4 -> 4; matrix products, arithmetic and copies ran while one was open for 1% -> 1% of each run, Pallas kernels for 9% -> 10%
where the time goes in v6:
time: 153 us; the launch traced here: 152 us
  blocking collectives  105 us (69%)
  Pallas kernels  20.1 us (13%)
  starting transfers between devices  17.8 us (12%)
  waiting for transfers between devices  6.93 us (5%)
  local copies, waits for them, and re-layouts  2.25 us (1%)
    all_to_all x7, blocking collectives, exchange(): return lax.all_to_all(array, axes, 0, 0, tiled=True)  105 us
    pallas_call x1, Pallas kernels, convolve(): pl.pallas_call(conv_kernel, grid=(2, steps), in_specs=[pl.BlockSpec((1, C...  12.1 us
    all_to_all x1, starting transfers between devices, exchange(): return lax.all_to_all(array, axes, 0, 0, tiled=True)  6.29 us
    ppermute x2, waiting for transfers between devices, from_neighbours(): lax.ppermute(high, axes, backward)  5.51 us
    ppermute x2, starting transfers between devices, from_neighbours(): lax.ppermute(low, axes, forward)  4.69 us
    ppermute x1, starting transfers between devices, on_device(): other = lax.ppermute(own, 'core', SWAP)  4.28 us
  transfers between devices with their start and end apart: 6, of which 4 were waited for; matrix products, arithmetic and copies ran while one was open for 1% of the time, Pallas kernels for 10%

profile of v6, /device:TPU:0, one launch (start us, length us, event | category | flops | bytes accessed | tf_op | source)
XLA Modules:
  0.0 152.5 jit_solution(7057749211708542835)
XLA Ops:
  0.0 1.4 fusion.10
  1.4 1.3 collective-permute-start
  2.8 1.3 collective-permute-start.1
  4.1 0.0 copy-start.3
  4.1 2.5 %pack.1 = bf16[4,2048,128]{2,1,0:T(8,128)(2,1)} custom-call(bf16[4,1024,128]{2,1,0:T(8,128)(2,1)} %bitcast.16, bf16[4,1024,128]{2,1,0:T(8,128)(2,1)} %bitcast.17), custom_call_target="tpu_custom_call" | custom-call | tf_op jit(solution)/shard_map/pack/pallas_call | solution.py:77
  6.5 0.0 collective-permute-done.left
  6.6 1.3 collective-permute-done.1.right
  7.8 6.3 %all-to-all-start = ((bf16[4,2048,128]{2,1,0:T(8,128)(2,1)}), bf16[4,2048,128]{2,1,0:T(8,128)(2,1)S(1)}, u32[]{:S(2)}, u32[]{:S(2)}) async-start(bf16[4,2048,128]{2,1,0:T(8,128)(2,1)} %pack.1), calls=%async_computation | async-start | bytes 4194304 | tf_op jit(solution)/shard_map/all_to_all | solution.py:409
  14.1 0.8 slice_bitcast_fusion
  14.9 3.4 %collective-permute-start.2 = (bf16[2,80,128]{2,1,0:T(8,128)(2,1)S(1)}, bf16[2,80,128]{2,1,0:T(8,128)(2,1)S(1)}, u32[]{:S(2)}, u32[]{:S(2)}) collective-permute-start(bf16[2,80,128]{2,1,0:T(8,128)(2,1)S(1)} %fusion.7), channel_id=1, source_target_pairs={{0,16},{16,32},{32,48},{48,64},{64,80},{80,96},{96,112},{1,17},{17... | collective-permute-start | bytes 122888 | tf_op jit(solution)/shard_map/ppermute | solution.py:415
  18.3 1.3 collective-permute-start.3
  19.6 0.3 collective-permute-done.2.top
  20.0 4.3 %collective-permute-done.3.bottom = bf16[2,80,128]{2,1,0:T(8,128)(2,1)S(1)} collective-permute-done((bf16[2,80,128]{2,1,0:T(8,128)(2,1)S(1)}, bf16[2,80,128]{2,1,0:T(8,128)(2,1)S(1)}, u32[]{:S(2)}, u32[]{:S(2)}) %collective-permute-start.3) | collective-permute-done | bytes 40992 | tf_op jit(solution)/shard_map/ppermute | solution.py:415
  24.2 0.0 copy-done.3
  24.2 12.1 %conv_block.1 = (bf16[2,128,4,16,128]{4,3,2,1,0:T(8,128)(2,1)}, bf16[64,32,128]{2,1,0:T(8,128)(2,1)S(1)}) custom-call(bf16[2,128,64,128]{3,2,1,0:T(8,128)(2,1)} %below.1, bf16[2,128,64,128]{3,2,1,0:T(8,128)(2,1)} %below.1, bf16[2,128,64,128]{3,2,1,0:T(8,128)(2,1)} %below.1, bf16[2,80,128]{2,1,0:T(8,128)(2,1)S(1)} %collective-permute-done.2.top, ...), custom_call_target="tpu_custom_call" | custom-call | flops 4831838208 | bytes 9437184 | tf_op jit(solution)/shard_map/conv_block/pallas_call | solution.py:177
  36.3 1.1 all-to-all-done.own
  37.4 0.0 copy-start.1
  37.4 4.3 %collective-permute-start.4 = (bf16[4,2048,128]{2,1,0:T(8,128)(2,1)S(1)}, bf16[4,2048,128]{2,1,0:T(8,128)(2,1)S(1)}, u32[]{:S(2)}, u32[]{:S(2)}) collective-permute-start(bf16[4,2048,128]{2,1,0:T(8,128)(2,1)S(1)} %all-to-all-done.own), channel_id=1, source_target_pairs={{0,1},{1,0},{2,3},{3,2},{4,5},{5,4},{6,7},{7,6},{8,9},{9,8},{10,11... | collective-permute-start | bytes 6291464 | tf_op jit(solution)/shard_map/ppermute | solution.py:434
  41.7 23.4 %all_to_all.40.received = bf16[64,32,128]{2,1,0:T(8,128)(2,1)S(1)} all-to-all(bf16[64,32,128]{2,1,0:T(8,128)(2,1)S(1)} %get-tuple-element.21), channel_id=1, replica_groups=mesh['z'=4,'xl'=2,'xh'=2,'y'=4,'core'=2] {'xh','y','z','xl'}, dimensions={0} | all-to-all | bytes 1048576 | tf_op jit(solution)/shard_map/all_to_all | solution.py:409
  65.0 0.0 copy-start.2
  65.0 0.0 collective-permute-done.4.other
  65.0 0.8 embed.1
  65.9 14.0 %all_to_all.41.terms = bf16[32,2,32,128]{3,2,1,0:T(8,128)(2,1)S(1)} all-to-all(bf16[32,2,32,128]{3,2,1,0:T(8,128)(2,1)S(1)} %embed.1), channel_id=1, replica_groups=mesh['z'=4,'xl'=2,'xh'=2,'y'=4,'core'=2] {'xl','y','z'}, dimensions={0} | all-to-all | bytes 1048576 | tf_op jit(solution)/shard_map/all_to_all | solution.py:409
  79.9 0.1 sum_and_copy.1
  80.0 13.6 %all_to_all.42.embedded = bf16[16,2,32,128]{3,2,1,0:T(8,128)(2,1)S(1)} all-to-all(bf16[16,2,32,128]{3,2,1,0:T(8,128)(2,1)S(1)} %get-tuple-element.23), channel_id=1, replica_groups=mesh['z'=4,'xl'=2,'xh'=2,'y'=4,'core'=2] {'core','y','xh'}, dimensions={0} | all-to-all | bytes 524288 | tf_op jit(solution)/shard_map/all_to_all | solution.py:409
  93.6 0.0 copy-done.1
  93.6 0.5 qkv.1
  94.1 9.7 %all_to_all.43.pairs = bf16[8,2,64,128]{3,2,1,0:T(8,128)(2,1)S(1)} all-to-all(bf16[8,2,64,128]{3,2,1,0:T(8,128)(2,1)S(1)} %get-tuple-element.25), channel_id=1, replica_groups=mesh['z'=4,'xl'=2,'xh'=2,'y'=4,'core'=2] {'z','xl'}, dimensions={0} | all-to-all | bytes 524288 | tf_op jit(solution)/shard_map/all_to_all | solution.py:409
  103.8 0.0 copy-done.2
  103.8 0.7 attend.1
  104.5 12.3 %all_to_all.44.terms = bf16[16,2,32,128]{3,2,1,0:T(8,128)(2,1)S(1)} all-to-all(bf16[16,2,32,128]{3,2,1,0:T(8,128)(2,1)S(1)} %attend.1), channel_id=1, replica_groups=mesh['z'=4,'xl'=2,'xh'=2,'y'=4,'core'=2] {'core','y','xh'}, dimensions={0} | all-to-all | bytes 524288 | tf_op jit(solution)/shard_map/all_to_all | solution.py:409
  116.8 0.0 copy-start
  116.8 0.1 mix_and_copy.1
  116.9 15.1 %all_to_all.45.mixed = bf16[32,2,32,128]{3,2,1,0:T(8,128)(2,1)S(1)} all-to-all(bf16[32,2,32,128]{3,2,1,0:T(8,128)(2,1)S(1)} %mix_and_copy.1), channel_id=1, replica_groups=mesh['z'=4,'xl'=2,'xh'=2,'y'=4,'core'=2] {'xl','z','y'}, dimensions={0} | all-to-all | bytes 1048576 | tf_op jit(solution)/shard_map/all_to_all | solution.py:409
  132.0 0.8 unembed.1
  132.8 17.1 %all_to_all.46.received = bf16[64,32,128]{2,1,0:T(8,128)(2,1)S(1)} all-to-all(bf16[64,32,128]{2,1,0:T(8,128)(2,1)S(1)} %unembed.1), channel_id=1, replica_groups=mesh['z'=4,'xl'=2,'xh'=2,'y'=4,'core'=2] {'y','xh','xl','z'}, dimensions={0} | all-to-all | bytes 1048576 | tf_op jit(solution)/shard_map/all_to_all | solution.py:409
  149.9 0.0 copy-done
  149.9 2.6 %finish.1 = bf16[2,128,64,128]{3,2,1,0:T(8,128)(2,1)} custom-call(bf16[2,128,4,16,128]{4,3,2,1,0:T(8,128)(2,1)S(1)} %copy-done, bf16[64,32,128]{2,1,0:T(8,128)(2,1)S(1)} %all_to_all.46.received), custom_call_target="tpu_custom_call" | custom-call | tf_op jit(solution)/shard_map/finish/pallas_call | solution.py:393
  (5 shorter events, 0.1 us)
Async XLA Ops:
  1.4 5.1 %collective-permute-start = (bf16[2,128,128]{2,1,0:T(8,128)(2,1)S(1)}, bf16[2,128,128]{2,1,0:T(8,128)(2,1)S(1)}, u32[]{:S(2)}, u32[]{:S(2)}) collective-permute-start(bf16[2,128,128]{2,1,0:T(8,128)(2,1)S(1)} %bitcast.18), channel_id=1, source_target_pairs={{0,1},{1,2},{2,3},{3,4},{4,5},{5,6},{6,7},{7,8},{8,9},{9,10},{10,1... | collective-permute-start | bytes 196616 | tf_op jit(solution)/shard_map/ppermute | solution.py:415
  2.8 5.0 %collective-permute-start.1 = (bf16[2,128,128]{2,1,0:T(8,128)(2,1)S(1)}, bf16[2,128,128]{2,1,0:T(8,128)(2,1)S(1)}, u32[]{:S(2)}, u32[]{:S(2)}) collective-permute-start(bf16[2,128,128]{2,1,0:T(8,128)(2,1)S(1)} %bitcast.19), channel_id=1, source_target_pairs={{1,0},{2,1},{3,2},{4,3},{5,4},{6,5},{7,6},{8,7},{9,8},{10,9},{11,1... | collective-permute-start | bytes 196616 | tf_op jit(solution)/shard_map/ppermute | solution.py:415
  4.1 20.2 %copy-start.3 = (bf16[3,3,128,128]{3,2,1,0:T(8,128)(2,1)S(1)}, bf16[3,3,128,128]{3,2,1,0:T(8,128)(2,1)}, u32[]{:S(2)}) copy-start(bf16[3,3,128,128]{3,2,1,0:T(8,128)(2,1)} %weight.3) | copy-start | bytes 884740
  7.8 29.6 %all-to-all-start = ((bf16[4,2048,128]{2,1,0:T(8,128)(2,1)}), bf16[4,2048,128]{2,1,0:T(8,128)(2,1)S(1)}, u32[]{:S(2)}, u32[]{:S(2)}) async-start(bf16[4,2048,128]{2,1,0:T(8,128)(2,1)} %pack.1), calls=%async_computation | async-start | bytes 4194304 | tf_op jit(solution)/shard_map/all_to_all | solution.py:409
  14.9 5.1 %collective-permute-start.2 = (bf16[2,80,128]{2,1,0:T(8,128)(2,1)S(1)}, bf16[2,80,128]{2,1,0:T(8,128)(2,1)S(1)}, u32[]{:S(2)}, u32[]{:S(2)}) collective-permute-start(bf16[2,80,128]{2,1,0:T(8,128)(2,1)S(1)} %fusion.7), channel_id=1, source_target_pairs={{0,16},{16,32},{32,48},{48,64},{64,80},{80,96},{96,112},{1,17},{17... | collective-permute-start | bytes 122888 | tf_op jit(solution)/shard_map/ppermute | solution.py:415
  18.3 5.9 %collective-permute-start.3 = (bf16[2,80,128]{2,1,0:T(8,128)(2,1)S(1)}, bf16[2,80,128]{2,1,0:T(8,128)(2,1)S(1)}, u32[]{:S(2)}, u32[]{:S(2)}) collective-permute-start(bf16[2,80,128]{2,1,0:T(8,128)(2,1)S(1)} %fusion.9), channel_id=1, source_target_pairs={{16,0},{32,16},{48,32},{64,48},{80,64},{96,80},{112,96},{17,1},{33... | collective-permute-start | bytes 122888 | tf_op jit(solution)/shard_map/ppermute | solution.py:415
  37.4 56.3 %copy-start.1 = (bf16[3,2048,128]{2,1,0:T(8,128)(2,1)S(1)}, bf16[3,2048,128]{2,1,0:T(8,128)(2,1)}, u32[]{:S(2)}) copy-start(bf16[3,2048,128]{2,1,0:T(8,128)(2,1)} %weight.4) | copy-start | bytes 4718596
  37.4 27.6 %collective-permute-start.4 = (bf16[4,2048,128]{2,1,0:T(8,128)(2,1)S(1)}, bf16[4,2048,128]{2,1,0:T(8,128)(2,1)S(1)}, u32[]{:S(2)}, u32[]{:S(2)}) collective-permute-start(bf16[4,2048,128]{2,1,0:T(8,128)(2,1)S(1)} %all-to-all-done.own), channel_id=1, source_target_pairs={{0,1},{1,0},{2,3},{3,2},{4,5},{5,4},{6,7},{7,6},{8,9},{9,8},{10,11... | collective-permute-start | bytes 6291464 | tf_op jit(solution)/shard_map/ppermute | solution.py:434
  65.0 38.8 %copy-start.2 = (bf16[128,2048]{1,0:T(8,128)(2,1)S(1)}, bf16[128,2048]{1,0:T(8,128)(2,1)}, u32[]{:S(2)}) copy-start(bf16[128,2048]{1,0:T(8,128)(2,1)} %weight.5) | copy-start | bytes 1572868
  116.8 33.1 %copy-start = (bf16[2,128,4,16,128]{4,3,2,1,0:T(8,128)(2,1)S(1)}, bf16[2,128,4,16,128]{4,3,2,1,0:T(8,128)(2,1)}, u32[]{:S(2)}) copy-start(bf16[2,128,4,16,128]{4,3,2,1,0:T(8,128)(2,1)} %get-tuple-element.18.features) | copy-start | bytes 12582916
